TPU v7x, 32 devices: a whole 2x2x4 slice. The times are simulated.
32 devices in a mesh: sec: 2 (over x), tile: 16 (over z, y, core).
Axes of the slice: x: 2, y: 2, z: 4, core: 2. Of those that a mesh axis runs over, the one named last changes fastest.
Arguments:
- prognostic_quantities: float32 [5, 128, 512, 256], P(None, None, 'tile', 'sec'), may hold values from -6 to 6
- advective_ratio: float32 [2, 128], replicated, may hold values from -0.35 to 0.35
- horizontal_diffuse_ratio: float32 [128], replicated, may hold values from 0.08 to 0.16
- upright_diffuse_ratio: float32 [128], replicated, may hold values from 0.03 to 0.15
- transfer_coefficient: float32 [512, 256], P('tile', 'sec'), may hold values from 0.05 to 0.3
- terrain_outer_warmth: float32 [512, 256], P('tile', 'sec'), may hold values from -6 to 6
- earlier_marine_warmth: float32 [512, 256], P('tile', 'sec'), may hold values from -6 to 6
- marine_indicator: int32 [512, 256], P('tile', 'sec'), may hold values 0 or 1
- marine_salinity_heat_vector: float32 [2, 80, 32768], P(None, None, ('sec', 'tile')), may hold values from -6 to 6
- marine_layer_diffuse_ratio: float32 [79], replicated, may hold values from 0.3 to 3
- group_active_extent: int32 [32], P(('sec', 'tile')), may hold values from 1 to 1024, 16384 in all
- intersect_air_site: int32 [4, 32768], P(None, ('sec', 'tile')), may hold values from 0 to 12287, as said below
- intersect_interpolation_share: float32 [4, 32768], P(None, ('sec', 'tile')), may hold values from 0.1 to 0.5
Outputs:
- new_tracers: float32 [5, 128, 512, 256], P(None, None, 'tile', 'sec')
- resolved_marine_properties: float32 [2, 80, 32768], P(None, None, ('sec', 'tile'))
- upcoming_marine_warmth: float32 [512, 256], P('tile', 'sec')
Inputs may be any that keep to these rules, and one draw needn't show every extreme that they name: `intersect_air_site`: in the columns of block b, entries below 4096 name a cell of tile b - 1, entries from 4096 to 8191 a cell of tile b, the rest a cell of tile b + 1; block 0 never names tile -1 and block 31 never names tile 32. Each block has 1024 column slots, of which the first group_active_extent are live; both ocean outputs are zero in the other slots, and some block is full.
All inputs are finite; a program needn't handle non-finite values. No bound on the sum of `marine_indicator` on one device may be relied on, other than what follows from the above.
Results may differ from a plain program's by a relative error of at most 0.00002.
Values sent between devices are 32-bit elements; how exact they have to be, the bound alone decides.
A program may use at most 192 MiB of HBM per device.

v0:
```python
import jax
import jax.numpy as jnp
from jax import lax
from jax.sharding import PartitionSpec as P

STEPS = 3


def from_partner(block, axis, apart):
    count = lax.axis_size(axis)
    route = []
    for low in range(count):
        high = low | 1 << apart
        if high != low and high < count:
            route += [(low, high), (high, low)]
    return lax.ppermute(block, axis, route)


def padded(block, sides, width):
    for axis, dim in sides:
        count = lax.axis_size(axis)
        forward = [(i, i + 1) for i in range(count - 1)]
        backward = [(target, source) for source, target in forward]
        low = lax.ppermute(
            lax.slice_in_dim(block, block.shape[dim] - width, None, axis=dim), axis, forward
        )
        high = lax.ppermute(lax.slice_in_dim(block, 0, width, axis=dim), axis, backward)
        block = jnp.concatenate([low, block, high], axis=dim)
    return block


def pad_columns(row_extended):
    edge_pair = jnp.stack([row_extended[:, :, :, 0], row_extended[:, :, :, -1]])
    partner = from_partner(edge_pair, "sec", 0)
    is_western = lax.axis_index("sec") == 0
    nothing = jnp.zeros_like(partner[0])
    west_column = jnp.where(is_western, nothing, partner[1])
    east_column = jnp.where(is_western, partner[0], nothing)
    return jnp.concatenate(
        [west_column[:, :, :, None], row_extended, east_column[:, :, :, None]], axis=3
    )


def march_forward(
    margin_extended,
    advective_ratio,
    horizontal_diffuse_ratio,
    upright_diffuse_ratio,
    transfer_coefficient,
    outer_warmth,
    humid_multiplier,
):
    quantity_matrices = margin_extended[:, :, 1:-1, 1:-1]
    north_cells = margin_extended[:, :, 2:, 1:-1]
    south_cells = margin_extended[:, :, :-2, 1:-1]
    east_cells = margin_extended[:, :, 1:-1, 2:]
    west_cells = margin_extended[:, :, 1:-1, :-2]
    east_west = advective_ratio[0][None, :, None, None]
    north_south = advective_ratio[1][None, :, None, None]
    spread = east_cells + west_cells + north_cells + south_cells - 4.0 * quantity_matrices
    carried = 0.5 * east_west * (east_cells - west_cells) + 0.5 * north_south * (
        north_cells - south_cells
    )
    level_above = jnp.concatenate([quantity_matrices[:, :1], quantity_matrices[:, :-1]], axis=1)
    level_below = jnp.concatenate([quantity_matrices[:, 1:], quantity_matrices[:, -1:]], axis=1)
    mixing = upright_diffuse_ratio[None, :, None, None] * (
        level_above + level_below - 2.0 * quantity_matrices
    )
    updated = (
        quantity_matrices
        + horizontal_diffuse_ratio[None, :, None, None] * spread
        - carried
        + mixing
    )
    floor_index = quantity_matrices[:, -1]
    thermal_transfer = transfer_coefficient * (outer_warmth - floor_index[0])
    humidity_transfer = (
        transfer_coefficient * humid_multiplier * (0.6 * outer_warmth - floor_index[1])
    )
    surface = jnp.stack(
        [
            thermal_transfer,
            humidity_transfer,
            jnp.zeros_like(thermal_transfer),
            -transfer_coefficient * floor_index[3],
            -transfer_coefficient * floor_index[4],
        ]
    )
    updated = jnp.concatenate([updated[:, :-1], updated[:, -1:] + surface[:, None]], axis=1)
    return (updated, thermal_transfer, humidity_transfer)


def tridiagonal(marine_layer_diffuse_ratio):
    zero_one = jnp.zeros((1,), marine_layer_diffuse_ratio.dtype)
    upper_mix = jnp.concatenate([marine_layer_diffuse_ratio, zero_one])
    lower_mix = jnp.concatenate([zero_one, marine_layer_diffuse_ratio])
    return (-lower_mix, 1.0 + upper_mix + lower_mix, -upper_mix)


def local(
    prognostic_quantities,
    advective_ratio,
    horizontal_diffuse_ratio,
    upright_diffuse_ratio,
    transfer_coefficient,
    terrain_outer_warmth,
    earlier_marine_warmth,
    marine_indicator,
    marine_salinity_heat_vector,
    marine_layer_diffuse_ratio,
    group_active_extent,
    intersect_air_site,
    intersect_interpolation_share,
):
    kinds, level_count, tile_rows, tile_cols = prognostic_quantities.shape
    cell_count = tile_rows * tile_cols
    marine_share = marine_indicator.astype(jnp.float32)
    outer_warmth = (
        marine_share * earlier_marine_warmth + (1.0 - marine_share) * terrain_outer_warmth
    )
    humid_multiplier = 0.3 + 0.7 * marine_share
    heat_total = jnp.zeros((tile_rows, tile_cols), jnp.float32)
    moist_total = jnp.zeros((tile_rows, tile_cols), jnp.float32)
    quantity_matrices = prognostic_quantities
    for repeat in range(STEPS):
        row_extended = padded(quantity_matrices, (("tile", 2),), 1)
        padded_tile = pad_columns(row_extended)
        quantity_matrices, thermal_transfer, humidity_transfer = march_forward(
            padded_tile,
            advective_ratio,
            horizontal_diffuse_ratio,
            upright_diffuse_ratio,
            transfer_coefficient,
            outer_warmth,
            humid_multiplier,
        )
        heat_total = heat_total + thermal_transfer
        moist_total = moist_total + humidity_transfer
    flux_pair = jnp.stack([heat_total.reshape(1, -1), moist_total.reshape(1, -1)])
    received = padded(flux_pair, ((("sec", "tile"), 1),), 1)
    flux_flat = received.reshape(2, 3 * cell_count)
    picked = flux_flat[:, intersect_air_site]
    forcing = jnp.sum(picked * intersect_interpolation_share[None], axis=1)
    right_side = (
        marine_salinity_heat_vector.at[0, 0].add(-0.5 * forcing[0]).at[1, 0].add(0.5 * forcing[1])
    )
    ocean_levels = marine_salinity_heat_vector.shape[1]
    lower_diag, main_diag, upper_diag = tridiagonal(marine_layer_diffuse_ratio)
    solved = lax.linalg.tridiagonal_solve(
        jnp.broadcast_to(lower_diag, (2, ocean_levels)),
        jnp.broadcast_to(main_diag, (2, ocean_levels)),
        jnp.broadcast_to(upper_diag, (2, ocean_levels)),
        right_side,
    )
    slot_count = marine_salinity_heat_vector.shape[2]
    live_slot = (jnp.arange(slot_count) < group_active_extent[0]).astype(jnp.float32)
    resolved_marine_properties = solved * live_slot[None, None]
    top_temp = resolved_marine_properties[0, 0]
    weighted = intersect_interpolation_share * live_slot[None]
    contrib_values = jnp.stack([weighted * top_temp[None], weighted]).reshape(2, -1)
    contrib = (
        jnp.zeros((2, 3 * cell_count), jnp.float32)
        .at[:, intersect_air_site.reshape(-1)]
        .add(contrib_values)
    )
    pieces = contrib.reshape(2, 3, cell_count)
    outgoing = jnp.stack([pieces[:, 0], pieces[:, 2]], axis=1)
    arrived = padded(outgoing, ((("sec", "tile"), 1),), 1)
    gathered_total = pieces[:, 1] + arrived[:, 0] + arrived[:, 3]
    upcoming_marine_warmth = (
        (gathered_total[0] + earlier_marine_warmth.reshape(-1)) / (gathered_total[1] + 1.0)
    ).reshape(tile_rows, tile_cols)
    return (quantity_matrices, resolved_marine_properties, upcoming_marine_warmth)


def solution(mesh):
    return jax.shard_map(
        local,
        mesh=mesh,
        in_specs=(
            P(None, None, "tile", "sec"),
            P(),
            P(),
            P(),
            P("tile", "sec"),
            P("tile", "sec"),
            P("tile", "sec"),
            P("tile", "sec"),
            P(None, None, ("sec", "tile")),
            P(),
            P(("sec", "tile")),
            P(None, ("sec", "tile")),
            P(None, ("sec", "tile")),
        ),
        out_specs=(P(None, None, "tile", "sec"), P(None, None, ("sec", "tile")), P("tile", "sec")),
        check_vma=False,
    )
```

profile of v0, /device:TPU:0, one launch (start us, length us, event | category | flops | bytes accessed | tf_op | source)
XLA Modules:
  0.0 532.2 jit_solution(14850780329709250627)
XLA Ops:
  0.6 2.0 copy.2007
  2.6 11.3 %copy.1283 = f32[5,128,32,128]{1,3,2,0:T(8,128)} copy(f32[5,128,32,128]{3,2,1,0:T(8,128)} %param.21) | data formatting | bytes 20971520 | tf_op args[0]
  13.9 1.1 fusion.529
  15.0 2.4 collective-permute-start
  17.4 1.3 collective-permute-start.1
  18.7 16.3 %fusion.530 = (f32[5,127,32,128]{1,3,2,0:T(8,128)}, f32[5,127,32,128]{1,3,2,0:T(8,128)}) fusion(f32[5,128,32,128]{1,3,2,0:T(8,128)} %copy.1283), kind=kLoop, calls=%fused_computation.912 | loop fusion | bytes 41615360 | tf_op jit(solution)/shard_map/slice | solution.py:65
  38.5 5.4 %copy.1285 = f32[5,1,32,128]{1,3,2,0:T(8,128)} copy(f32[5,1,32,128]{3,2,1,0:T(8,128)S(1)} %get-tuple-element.782) | data formatting | bytes 163840 | tf_op jit(solution)/shard_map/slice | solution.py:64
  43.8 5.3 %copy.1287 = f32[5,1,32,128]{1,3,2,0:T(8,128)} copy(f32[5,1,32,128]{3,2,1,0:T(8,128)S(1)} %get-tuple-element.781) | data formatting | bytes 163840 | tf_op jit(solution)/shard_map/slice | solution.py:65
  52.1 5.4 %copy.1289 = f32[5,1,32,128]{1,3,2,0:T(8,128)} copy(f32[5,1,32,128]{3,2,0,1:T(8,128)S(1)} %bitcast.1931) | data formatting | bytes 163840 | tf_op jit(solution)/shard_map/broadcast_in_dim | solution.py:89
  62.8 1.4 maximum_bitcast_fusion.2
  64.4 2.4 collective-permute-start.2
  66.8 3.4 collective-permute-done.2
  70.4 39.1 %fusion.322 = f32[5,128,32,128]{1,3,2,0:T(8,128)S(1)} fusion(f32[5,127,32,128]{1,3,2,0:T(8,128)} %get-tuple-element.780, f32[5,1,32,128]{1,3,2,0:T(8,128)} %copy.1285, f32[5,1,32,128]{1,3,2,0:T(8,128)} %copy.1287, f32[5,127,32,128]{1,3,2,0:T(8,128)} %get-tuple-element.779, f32[5,128,32,128]{1,3,2,0:T(8,128)} %copy.1283, ...), kind=kLoop, calls=%fused_computation.652 | loop fusion | flops 73400320 | bytes 42774528 | tf_op jit(solution)/shard_map/add | solution.py:70
  109.5 14.8 %fusion.528 = (f32[5,1,32,128]{1,3,2,0:T(8,128)}, f32[5,1,32,128]{1,3,2,0:T(8,128)}) fusion(f32[5,128,32,128]{1,3,2,0:T(8,128)S(1)} %fusion.322, f32[5,1,32,128]{1,3,2,0:T(8,128)} %copy.1289), kind=kLoop, calls=%fused_computation.910 | loop fusion | flops 20480 | bytes 409600 | tf_op jit(solution)/shard_map/slice | solution.py:64
  124.4 5.7 %slice_reduce_fusion.4 = (f32[32,128]{1,0:T(8,128)S(1)}, f32[32,128]{1,0:T(8,128)S(1)}, f32[32,128]{1,0:T(8,128)S(1)}, f32[32,128]{1,0:T(8,128)S(1)}) fusion(f32[5,1,32,128]{1,3,2,0:T(8,128)} %get-tuple-element.776), kind=kLoop, calls=%fused_computation.676 | loop fusion | bytes 131072 | tf_op jit(solution)/shard_map/slice | solution.py:86
  130.1 1.3 fusion.336
  131.4 3.7 collective-permute-start.3
  135.2 1.8 collective-permute-start.4
  137.0 16.4 %slice_maximum_fusion.1 = f32[5,127,32,128]{1,3,2,0:T(8,128)} fusion(f32[5,1,32,128]{1,3,2,0:T(8,128)} %get-tuple-element.776, f32[5,127,32,128]{1,3,2,0:T(8,128)} %bitcast.1910), kind=kLoop, calls=%fused_computation.627 | loop fusion | flops 2600960 | bytes 20889600 | tf_op jit(solution)/shard_map/concatenate | solution.py:89
  153.4 2.1 maximum_bitcast_fusion.1
  155.7 2.0 collective-permute-start.5
  157.7 5.5 %copy.1290 = f32[5,1,32,128]{1,3,2,0:T(8,128)} copy(f32[5,1,32,128]{3,2,0,1:T(8,128)S(1)} %bitcast.1933) | data formatting | bytes 163840 | tf_op jit(solution)/shard_map/broadcast_in_dim | solution.py:89
  163.4 60.9 %fusion.325 = f32[5,128,32,128]{1,3,2,0:T(8,128)} fusion(f32[5,127,32,128]{1,3,2,0:T(8,128)} %bitcast.1912, f32[5,1,32,128]{1,3,2,0:T(8,128)} %get-tuple-element.775, f32[5,127,32,128]{1,3,2,0:T(8,128)} %slice_maximum_fusion.1, f32[5,1,32,128]{1,3,2,0:T(8,128)} %get-tuple-element.776, f32[5,128,1,128]{1,3,2,0:T(8,128)S(1)} %collective-permute-done.3, ...), kind=kLoop, calls=%fused_computation.656 | loop fusion | flops 86507520 | bytes 32288768 | tf_op jit(solution)/shard_map/add | solution.py:70
  224.2 15.6 %fusion.527 = (f32[5,1,32,128]{1,3,2,0:T(8,128)}, f32[5,1,32,128]{1,3,2,0:T(8,128)S(1)}) fusion(f32[5,128,32,128]{1,3,2,0:T(8,128)} %fusion.325, f32[5,1,32,128]{1,3,2,0:T(8,128)} %copy.1290), kind=kLoop, calls=%fused_computation.909 | loop fusion | flops 20480 | bytes 409600 | tf_op jit(solution)/shard_map/slice | solution.py:64
  239.8 2.6 slice_reduce_fusion
  242.4 1.0 add_add_fusion.2
  244.0 1.3 collective-permute-start.10
  245.3 6.9 %collective-permute-start.9 = (f32[2,1,4096]{2,0,1:T(2,128)}, f32[2,1,4096]{2,0,1:T(2,128)}, u32[]{:S(2)}, u32[]{:S(2)}) collective-permute-start(f32[2,1,4096]{2,0,1:T(2,128)} %pad_maximum_fusion.45), channel_id=1, source_target_pairs={{0,1},{1,2},{2,3},{3,4},{4,5},{5,6},{6,7},{7,8},{8,9},{9,10},{10,1... | collective-permute-start | bytes 98312 | tf_op jit(solution)/shard_map/ppermute | solution.py:24
  252.3 1.1 fusion.334
  253.4 16.4 %slice_maximum_fusion = f32[5,127,32,128]{1,3,2,0:T(8,128)} fusion(f32[5,1,32,128]{1,3,2,0:T(8,128)} %copy-done.2, f32[5,127,32,128]{1,3,2,0:T(8,128)} %bitcast.1905), kind=kLoop, calls=%fused_computation.613 | loop fusion | flops 2600960 | bytes 20889600 | tf_op jit(solution)/shard_map/concatenate | solution.py:89
  269.9 3.5 collective-permute-start.6
  273.4 1.3 collective-permute-start.7
  275.6 4.0 copy.1294
  279.6 15.5 %gather_fusion = f32[4096,2]{1,0:T(8,128)S(1)} fusion(f32[2,12288]{0,1:T(8,128)} %bitcast.1917, s32[4096]{0:T(1024)} %bitcast_clamp_fusion), kind=kCustom, calls=%fused_computation | custom fusion | bytes 81920 | tf_op jit(solution)/shard_map/gather | solution.py:142
  295.1 1.4 multiply_reduce_fusion
  300.9 17.3 %while.34 = (s32[]{:T(128)}, f32[2]{0:T(128)S(1)}, f32[2,1024]{1,0:T(2,128)S(1)}, f32[2,32,2]{1,0,2:T(2,128)}, f32[2,32,2,1024]{3,2,1,0:T(2,128)}, /*index=5*/f3...) while((s32[]{:T(128)}, f32[2]{0:T(128)S(1)}, ...), condition=%wide.region_2.3_spmd, body=%wide.region_1.2_spmd.sunk | while | flops 295137 | bytes 2157273 | solution.py:149
  308.4 1.2 dynamic_update_slice.23
  317.0 1.2 dynamic_update_slice.23
  318.2 27.3 %multiply_subtract_fusion = (f32[2]{0:T(128)S(1)}, f32[2]{0:T(128)S(1)}, f32[2]{0:T(128)S(1)}, f32[2]{0:T(128)S(1)}, f32[2]{0:T(128)S(1)}, /*index=5*/f32[2]{0:T...) fusion(f32[]{:T(128)} %bitcast.352, ...), kind=kLoop, calls=%fused_computation.875 | loop fusion | flops 88 | bytes 416 | tf_op jit(solution)/shard_map/vmap()/eval_jaxpr/sub | solution.py:149
  348.3 1.1 constant_dynamic-update-slice_fusion.94
  350.1 1.3 constant_dynamic-update-slice_fusion.91
  352.2 1.4 constant_dynamic-update-slice_fusion.89
  353.6 1.9 constant_dynamic-update-slice_fusion.88
  356.3 1.3 constant_dynamic-update-slice_fusion.86
  358.3 1.4 constant_dynamic-update-slice_fusion.84
  360.4 1.3 constant_dynamic-update-slice_fusion.82
  362.4 1.3 constant_dynamic-update-slice_fusion.80
  364.5 1.4 fusion.392
  366.0 3.8 while.35
  369.8 1.0 fusion.364
  372.7 25.6 %scatter_custom_fusion = f32[2,12288]{0,1:T(8,128)} fusion(s32[4096]{0:T(1024)} %bitcast.1957, f32[4096,2]{1,0:T(8,128)S(1)} %copy.1342, f32[]{:T(128)} %constant.140.clone.1), kind=kCustom, calls=%fused_computation.670 | custom fusion | flops 8192 | bytes 98816 | tf_op jit(solution)/shard_map/scatter-add | solution.py:164
  398.2 5.3 fusion.532
  403.5 2.2 copy.1370
  405.7 3.0 collective-permute-start.11
  408.7 2.2 copy.1371
  410.9 1.5 collective-permute-start.12
  412.4 5.4 %copy.1291 = f32[5,1,32,128]{1,3,2,0:T(8,128)} copy(f32[5,1,32,128]{3,2,0,1:T(8,128)S(1)} %bitcast.1932) | data formatting | bytes 163840 | tf_op jit(solution)/shard_map/broadcast_in_dim | solution.py:89
  418.6 2.1 maximum_bitcast_fusion
  420.9 7.7 %collective-permute-start.8 = (f32[2,5,128,34]{2,0,3,1:T(2,128)S(1)}, f32[2,5,128,34]{2,0,3,1:T(2,128)S(1)}, u32[]{:S(2)}, u32[]{:S(2)}) collective-permute-start(f32[2,5,128,34]{2,0,3,1:T(2,128)S(1)} %pad_maximum_fusion.35), channel_id=1, source_target_pairs={{0,16},{16,0},{1,17},{17,1},{2,18},{18,2},{3,19},{19,3},{4,20},{20... | collective-permute-start | bytes 522248 | tf_op jit(solution)/shard_map/ppermute | solution.py:16
  429.3 2.8 collective-permute-done.8
  432.2 59.7 %fusion.328 = f32[5,128,32,128]{1,3,2,0:T(8,128)} fusion(f32[5,127,32,128]{1,3,2,0:T(8,128)} %bitcast.1907, f32[5,1,32,128]{1,3,2,0:T(8,128)} %get-tuple-element.773, f32[5,127,32,128]{1,3,2,0:T(8,128)} %slice_maximum_fusion, f32[5,1,32,128]{1,3,2,0:T(8,128)} %copy-done.2, f32[5,128,1,128]{1,3,2,0:T(8,128)S(1)} %collective-permute-done.6, ...), kind=kLoop, calls=%fused_computation.660 | loop fusion | flops 86507520 | bytes 32288768 | tf_op jit(solution)/shard_map/add | solution.py:70
  492.0 14.4 %slice_add_fusion = f32[5,1,32,128]{1,3,2,0:T(8,128)} fusion(f32[5,1,32,128]{1,3,2,0:T(8,128)} %copy.1291, f32[5,128,32,128]{1,3,2,0:T(8,128)} %fusion.328), kind=kLoop, calls=%fused_computation.612 | loop fusion | flops 20480 | bytes 245760 | tf_op jit(solution)/shard_map/add | solution.py:89
  506.4 14.3 %pad_maximum_fusion.32 = f32[5,128,32,128]{1,3,2,0:T(8,128)} fusion(f32[5,1,32,128]{1,3,2,0:T(8,128)} %slice_add_fusion, f32[5,127,32,128]{1,3,2,0:T(8,128)} %bitcast.1913), kind=kLoop, calls=%fused_computation.661 | loop fusion | flops 2621440 | bytes 20971520 | tf_op jit(solution)/shard_map/concatenate | solution.py:89
  520.7 11.3 %copy.1346 = f32[5,128,32,128]{3,2,1,0:T(8,128)} copy(f32[5,128,32,128]{1,3,2,0:T(8,128)} %pad_maximum_fusion.32) | data formatting | bytes 20971520
  (413 shorter events, 45.8 us)
Async XLA Ops:
  15.0 47.8 %collective-permute-start = (f32[5,128,1,128]{1,3,2,0:T(8,128)S(1)}, f32[5,128,1,128]{1,3,2,0:T(8,128)S(1)}, u32[]{:S(2)}, u32[]{:S(2)}) collective-permute-start(f32[5,128,1,128]{1,3,2,0:T(8,128)S(1)} %get-tuple-element.778), channel_id=1, source_target_pairs={{0,1},{1,2},{2,3},{3,4},{4,5},{5,6},{6,7},{7,8},{8,9},{9,10},{10,1... | collective-permute-start | bytes 983048 | tf_op jit(solution)/shard_map/ppermute | solution.py:24
  17.4 45.4 %collective-permute-start.1 = (f32[5,128,1,128]{1,3,2,0:T(8,128)S(1)}, f32[5,128,1,128]{1,3,2,0:T(8,128)S(1)}, u32[]{:S(2)}, u32[]{:S(2)}) collective-permute-start(f32[5,128,1,128]{1,3,2,0:T(8,128)S(1)} %get-tuple-element.777), channel_id=1, source_target_pairs={{1,0},{2,1},{3,2},{4,3},{5,4},{6,5},{7,6},{8,7},{9,8},{10,9},{11,1... | collective-permute-start | bytes 983048 | tf_op jit(solution)/shard_map/ppermute | solution.py:27
  18.7 17.3 %copy-start.35 = (f32[79]{0:T(128)S(1)}, f32[79]{0:T(128)}, u32[]{:S(2)}) copy-start(f32[79]{0:T(128)} %param.30) | copy-start | bytes 952
  38.4 10.8 %copy-start.4 = (f32[32,128]{1,0:T(8,128)S(1)}, f32[32,128]{1,0:T(8,128)}, u32[]{:S(2)}) copy-start(f32[32,128]{1,0:T(8,128)} %param.25) | copy-start | bytes 49156
  38.4 10.8 %copy-start.23 = (s32[32,128]{1,0:T(8,128)S(1)}, s32[32,128]{1,0:T(8,128)}, u32[]{:S(2)}) copy-start(s32[32,128]{1,0:T(8,128)} %param.28) | copy-start | bytes 49156
  38.4 10.8 %copy-start.25 = (f32[32,128]{1,0:T(8,128)S(1)}, f32[32,128]{1,0:T(8,128)}, u32[]{:S(2)}) copy-start(f32[32,128]{1,0:T(8,128)} %param.27) | copy-start | bytes 49156
  38.4 10.7 %copy-start.27 = (f32[32,128]{1,0:T(8,128)S(1)}, f32[32,128]{1,0:T(8,128)}, u32[]{:S(2)}) copy-start(f32[32,128]{1,0:T(8,128)} %param.26) | copy-start | bytes 49156
  43.8 13.7 %copy-start.24 = (s32[4,1024]{1,0:T(4,128)S(1)}, s32[4,1024]{1,0:T(4,128)}, u32[]{:S(2)}) copy-start(s32[4,1024]{1,0:T(4,128)} %param.32) | copy-start | bytes 49156
  50.7 86.3 %copy-start.6 = (f32[32,128]{1,0:T(8,128)}, f32[32,128]{1,0:T(8,128)S(1)}, u32[]{:S(2)}) copy-start(f32[32,128]{1,0:T(8,128)S(1)} %get-tuple-element.678) | copy-start | bytes 49156
  52.1 14.7 %copy-start.34 = (f32[2,128]{1,0:T(2,128)S(1)}, f32[2,128]{1,0:T(2,128)}, u32[]{:S(2)}) copy-start(f32[2,128]{1,0:T(2,128)} %param.22) | copy-start | bytes 3076
  52.1 18.2 %copy-start.30 = (f32[128]{0:T(128)S(1)}, f32[128]{0:T(128)}, u32[]{:S(2)}) copy-start(f32[128]{0:T(128)} %param.24) | copy-start | bytes 1540
  52.1 18.2 %copy-start.32 = (f32[128]{0:T(128)S(1)}, f32[128]{0:T(128)}, u32[]{:S(2)}) copy-start(f32[128]{0:T(128)} %param.23) | copy-start | bytes 1540
  64.4 5.8 %collective-permute-start.2 = (f32[2,5,128,34]{2,0,3,1:T(2,128)S(1)}, f32[2,5,128,34]{2,0,3,1:T(2,128)S(1)}, u32[]{:S(2)}, u32[]{:S(2)}) collective-permute-start(f32[2,5,128,34]{2,0,3,1:T(2,128)S(1)} %pad_maximum_fusion.33), channel_id=1, source_target_pairs={{0,16},{16,0},{1,17},{17,1},{2,18},{18,2},{3,19},{19,3},{4,20},{20... | collective-permute-start | bytes 522248 | tf_op jit(solution)/shard_map/ppermute | solution.py:16
  66.8 96.5 %copy-start.28 = (f32[128]{0:T(128)}, f32[128]{0:T(128)S(1)}, u32[]{:S(2)}) copy-start(f32[128]{0:T(128)S(1)} %get-tuple-element.812) | copy-start | bytes 1540
  109.5 20.6 %copy-start.1 = (f32[5,128,32,128]{1,3,2,0:T(8,128)}, f32[5,128,32,128]{1,3,2,0:T(8,128)S(1)}, u32[]{:S(2)}) copy-start(f32[5,128,32,128]{1,3,2,0:T(8,128)S(1)} %fusion.322) | copy-start | bytes 31457284
  130.1 6.8 %copy-start.9 = (f32[32,128]{1,0:T(8,128)}, f32[32,128]{1,0:T(8,128)S(1)}, u32[]{:S(2)}) copy-start(f32[32,128]{1,0:T(8,128)S(1)} %get-tuple-element.448) | copy-start | bytes 49156
  130.1 6.9 %copy-start.8 = (f32[32,128]{1,0:T(8,128)}, f32[32,128]{1,0:T(8,128)S(1)}, u32[]{:S(2)}) copy-start(f32[32,128]{1,0:T(8,128)S(1)} %get-tuple-element.447) | copy-start | bytes 49156
  131.4 21.9 %collective-permute-start.3 = (f32[5,128,1,128]{1,3,2,0:T(8,128)S(1)}, f32[5,128,1,128]{1,3,2,0:T(8,128)S(1)}, u32[]{:S(2)}, u32[]{:S(2)}) collective-permute-start(f32[5,128,1,128]{1,3,2,0:T(8,128)S(1)} %get-tuple-element.768), channel_id=1, source_target_pairs={{0,1},{1,2},{2,3},{3,4},{4,5},{5,6},{6,7},{7,8},{8,9},{9,10},{10,1... | collective-permute-start | bytes 983048 | tf_op jit(solution)/shard_map/ppermute | solution.py:24
  135.2 18.2 %collective-permute-start.4 = (f32[5,128,1,128]{1,3,2,0:T(8,128)S(1)}, f32[5,128,1,128]{1,3,2,0:T(8,128)S(1)}, u32[]{:S(2)}, u32[]{:S(2)}) collective-permute-start(f32[5,128,1,128]{1,3,2,0:T(8,128)S(1)} %get-tuple-element.767), channel_id=1, source_target_pairs={{1,0},{2,1},{3,2},{4,3},{5,4},{6,5},{7,6},{8,7},{9,8},{10,9},{11,1... | collective-permute-start | bytes 983048 | tf_op jit(solution)/shard_map/ppermute | solution.py:27
  155.7 7.5 %collective-permute-start.5 = (f32[2,5,128,34]{2,0,3,1:T(2,128)S(1)}, f32[2,5,128,34]{2,0,3,1:T(2,128)S(1)}, u32[]{:S(2)}, u32[]{:S(2)}) collective-permute-start(f32[2,5,128,34]{2,0,3,1:T(2,128)S(1)} %pad_maximum_fusion.34), channel_id=1, source_target_pairs={{0,16},{16,0},{1,17},{17,1},{2,18},{18,2},{3,19},{19,3},{4,20},{20... | collective-permute-start | bytes 522248 | tf_op jit(solution)/shard_map/ppermute | solution.py:16
  224.2 28.1 %copy-start = (f32[5,128,32,128]{1,3,2,0:T(8,128)S(1)}, f32[5,128,32,128]{1,3,2,0:T(8,128)}, u32[]{:S(2)}) copy-start(f32[5,128,32,128]{1,3,2,0:T(8,128)} %fusion.325) | copy-start | bytes 31457284
  239.8 12.4 %copy-start.2 = (f32[5,1,32,128]{1,3,2,0:T(8,128)}, f32[5,1,32,128]{1,3,2,0:T(8,128)S(1)}, u32[]{:S(2)}) copy-start(f32[5,1,32,128]{1,3,2,0:T(8,128)S(1)} %get-tuple-element.774) | copy-start | bytes 245764
  242.4 9.9 %copy-start.10 = (f32[32,128]{1,0:T(8,128)}, f32[32,128]{1,0:T(8,128)S(1)}, u32[]{:S(2)}) copy-start(f32[32,128]{1,0:T(8,128)S(1)} %get-tuple-element.443) | copy-start | bytes 49156
  242.4 9.9 %copy-start.12 = (f32[32,128]{1,0:T(8,128)}, f32[32,128]{1,0:T(8,128)S(1)}, u32[]{:S(2)}) copy-start(f32[32,128]{1,0:T(8,128)S(1)} %get-tuple-element.444) | copy-start | bytes 49156
  243.4 8.9 %copy-start.14 = (f32[32,128]{1,0:T(8,128)}, f32[32,128]{1,0:T(8,128)S(1)}, u32[]{:S(2)}) copy-start(f32[32,128]{1,0:T(8,128)S(1)} %get-tuple-element.771) | copy-start | bytes 49156
  243.4 8.9 %copy-start.16 = (f32[32,128]{1,0:T(8,128)}, f32[32,128]{1,0:T(8,128)S(1)}, u32[]{:S(2)}) copy-start(f32[32,128]{1,0:T(8,128)S(1)} %get-tuple-element.772) | copy-start | bytes 49156
  244.0 30.7 %collective-permute-start.10 = (f32[2,1,4096]{2,0,1:T(2,128)}, f32[2,1,4096]{2,0,1:T(2,128)}, u32[]{:S(2)}, u32[]{:S(2)}) collective-permute-start(f32[2,1,4096]{2,0,1:T(2,128)} %pad_maximum_fusion.45), channel_id=1, source_target_pairs={{1,0},{2,1},{3,2},{4,3},{5,4},{6,5},{7,6},{8,7},{9,8},{10,9},{11,1... | collective-permute-start | bytes 98312 | tf_op jit(solution)/shard_map/ppermute | solution.py:27
  245.3 29.4 %collective-permute-start.9 = (f32[2,1,4096]{2,0,1:T(2,128)}, f32[2,1,4096]{2,0,1:T(2,128)}, u32[]{:S(2)}, u32[]{:S(2)}) collective-permute-start(f32[2,1,4096]{2,0,1:T(2,128)} %pad_maximum_fusion.45), channel_id=1, source_target_pairs={{0,1},{1,2},{2,3},{3,4},{4,5},{5,6},{6,7},{7,8},{8,9},{9,10},{10,1... | collective-permute-start | bytes 98312 | tf_op jit(solution)/shard_map/ppermute | solution.py:24
  253.4 16.5 %copy-start.13 = (f32[32,128]{1,0:T(8,128)S(1)}, f32[32,128]{1,0:T(8,128)}, u32[]{:S(2)}) copy-start(f32[32,128]{1,0:T(8,128)} %copy-done.12) | copy-start | bytes 49156
  253.4 21.3 %copy-start.7 = (f32[32,128]{1,0:T(8,128)S(1)}, f32[32,128]{1,0:T(8,128)}, u32[]{:S(2)}) copy-start(f32[32,128]{1,0:T(8,128)} %copy-done.6) | copy-start | bytes 49156
  253.4 21.3 %copy-start.11 = (f32[32,128]{1,0:T(8,128)S(1)}, f32[32,128]{1,0:T(8,128)}, u32[]{:S(2)}) copy-start(f32[32,128]{1,0:T(8,128)} %copy-done.10) | copy-start | bytes 49156
  253.4 21.3 %copy-start.22 = (f32[32,128]{1,0:T(8,128)S(1)}, f32[32,128]{1,0:T(8,128)}, u32[]{:S(2)}) copy-start(f32[32,128]{1,0:T(8,128)} %get-tuple-element.442) | copy-start | bytes 49156
  253.4 21.4 %copy-start.15 = (f32[32,128]{1,0:T(8,128)S(1)}, f32[32,128]{1,0:T(8,128)}, u32[]{:S(2)}) copy-start(f32[32,128]{1,0:T(8,128)} %copy-done.14) | copy-start | bytes 49156
  253.4 21.4 %copy-start.17 = (f32[32,128]{1,0:T(8,128)S(1)}, f32[32,128]{1,0:T(8,128)}, u32[]{:S(2)}) copy-start(f32[32,128]{1,0:T(8,128)} %copy-done.16) | copy-start | bytes 49156
  269.9 27.2 %copy-start.3 = (f32[2,80,1024]{2,1,0:T(8,128)S(1)}, f32[2,80,1024]{2,1,0:T(8,128)}, u32[]{:S(2)}) copy-start(f32[2,80,1024]{2,1,0:T(8,128)} %copy.2007) | copy-start | bytes 1966084
  269.9 148.7 %collective-permute-start.6 = (f32[5,128,1,128]{1,3,2,0:T(8,128)}, f32[5,128,1,128]{1,3,2,0:T(8,128)S(1)}, u32[]{:S(2)}, u32[]{:S(2)}) collective-permute-start(f32[5,128,1,128]{1,3,2,0:T(8,128)} %get-tuple-element.766), channel_id=1, source_target_pairs={{0,1},{1,2},{2,3},{3,4},{4,5},{5,6},{6,7},{7,8},{8,9},{9,10},{10,1... | collective-permute-start | bytes 983048 | tf_op jit(solution)/shard_map/ppermute | solution.py:24
  273.4 145.2 %collective-permute-start.7 = (f32[5,128,1,128]{1,3,2,0:T(8,128)}, f32[5,128,1,128]{1,3,2,0:T(8,128)S(1)}, u32[]{:S(2)}, u32[]{:S(2)}) collective-permute-start(f32[5,128,1,128]{1,3,2,0:T(8,128)} %get-tuple-element.765), channel_id=1, source_target_pairs={{1,0},{2,1},{3,2},{4,3},{5,4},{6,5},{7,6},{8,7},{9,8},{10,9},{11,1... | collective-permute-start | bytes 983048 | tf_op jit(solution)/shard_map/ppermute | solution.py:27
  274.7 4.9 copy-start.18
  318.2 53.6 %copy-start.20 = (f32[4,1024]{1,0:T(4,128)S(1)}, f32[4,1024]{1,0:T(4,128)}, u32[]{:S(2)}) copy-start(f32[4,1024]{1,0:T(4,128)} %param.33) | copy-start | bytes 49156
  371.8 31.6 %copy-start.5 = (f32[2,80,1024]{2,1,0:T(8,128)}, f32[2,80,1024]{2,1,0:T(8,128)S(1)}, u32[]{:S(2)}) copy-start(f32[2,80,1024]{2,1,0:T(8,128)S(1)} %maximum_multiply_fusion) | copy-start | bytes 1966084
  372.6 39.8 %copy-start.19 = (f32[5,32,128]{2,1,0:T(8,128)S(1)}, f32[5,32,128]{2,1,0:T(8,128)}, u32[]{:S(2)}) copy-start(f32[5,32,128]{2,1,0:T(8,128)} %copy-done.18) | copy-start | bytes 245764
  372.6 39.8 %copy-start.21 = (f32[32,128]{1,0:T(8,128)S(1)}, f32[32,128]{1,0:T(8,128)}, u32[]{:S(2)}) copy-start(f32[32,128]{1,0:T(8,128)} %get-tuple-element.441) | copy-start | bytes 49156
  405.7 12.7 %collective-permute-start.11 = (f32[2,1,4096]{2,1,0:T(1,128)S(1)}, f32[2,1,4096]{2,1,0:T(1,128)S(1)}, u32[]{:S(2)}, u32[]{:S(2)}) collective-permute-start(f32[2,1,4096]{2,1,0:T(1,128)S(1)} %copy.1370), channel_id=1, source_target_pairs={{0,1},{1,2},{2,3},{3,4},{4,5},{5,6},{6,7},{7,8},{8,9},{9,10},{10,1... | collective-permute-start | bytes 98312 | tf_op jit(solution)/shard_map/ppermute | solution.py:24
  410.9 7.5 %collective-permute-start.12 = (f32[2,1,4096]{2,1,0:T(1,128)S(1)}, f32[2,1,4096]{2,1,0:T(1,128)S(1)}, u32[]{:S(2)}, u32[]{:S(2)}) collective-permute-start(f32[2,1,4096]{2,1,0:T(1,128)S(1)} %copy.1371), channel_id=1, source_target_pairs={{1,0},{2,1},{3,2},{4,3},{5,4},{6,5},{7,6},{8,7},{9,8},{10,9},{11,1... | collective-permute-start | bytes 98312 | tf_op jit(solution)/shard_map/ppermute | solution.py:27
  418.5 10.1 %copy-start.26 = (f32[32,128]{1,0:T(8,128)S(1)}, f32[32,128]{1,0:T(8,128)}, u32[]{:S(2)}) copy-start(f32[32,128]{1,0:T(8,128)} %param.27) | copy-start | bytes 49156
  418.5 13.7 %copy-start.29 = (f32[128]{0:T(128)S(1)}, f32[128]{0:T(128)}, u32[]{:S(2)}) copy-start(f32[128]{0:T(128)} %copy-done.28) | copy-start | bytes 1540
  418.5 13.7 %copy-start.31 = (f32[128]{0:T(128)S(1)}, f32[128]{0:T(128)}, u32[]{:S(2)}) copy-start(f32[128]{0:T(128)} %param.24) | copy-start | bytes 1540
  418.6 13.7 %copy-start.33 = (f32[128]{0:T(128)S(1)}, f32[128]{0:T(128)}, u32[]{:S(2)}) copy-start(f32[128]{0:T(128)} %param.23) | copy-start | bytes 1540
  420.9 11.1 %collective-permute-start.8 = (f32[2,5,128,34]{2,0,3,1:T(2,128)S(1)}, f32[2,5,128,34]{2,0,3,1:T(2,128)S(1)}, u32[]{:S(2)}, u32[]{:S(2)}) collective-permute-start(f32[2,5,128,34]{2,0,3,1:T(2,128)S(1)} %pad_maximum_fusion.35), channel_id=1, source_target_pairs={{0,16},{16,0},{1,17},{17,1},{2,18},{18,2},{3,19},{19,3},{4,20},{20... | collective-permute-start | bytes 522248 | tf_op jit(solution)/shard_map/ppermute | solution.py:16
where the time goes:
time: 542 us; the launch traced here: 532 us
  other arithmetic  350 us (65%)
  local copies, waits for them, and re-layouts  133 us (25%)
  starting transfers between devices  38.7 us (7%)
  waiting for transfers between devices  6.21 us (1%)
    add x3, other arithmetic, march_forward(): quantity_matrices + horizontal_diffuse_ratio[None, :, None, None] * spread  160 us
    concatenate x5, other arithmetic, march_forward(): jnp.concatenate([updated[:, :-1], updated[:, -1:] + surface[:, None]], ax...  49.5 us
    unnamed x87, local copies, waits for them, and re-layouts  30.9 us
    slice x2, other arithmetic, march_forward(): quantity_matrices[:, :1]  30.4 us
    sub x3, other arithmetic, local(): lax.linalg.tridiagonal_solve(jnp.broadcast_to(lower_diag, (2, ocean_level...  27.4 us
    scatter-add x1, other arithmetic, local(): contrib = jnp.zeros((2, 3 * cell_count), jnp.float32).at[:, intersect_air...  25.6 us
    ppermute x5, starting transfers between devices, padded(): lax.ppermute(lax.slice_in_dim(block, block.shape[dim] - width, None, axis...  19.5 us
    unnamed x24, other arithmetic  16.5 us
  transfers between devices with their start and end apart: 13, of which 2 were waited for; matrix products, arithmetic and copies ran while one was open for 41% of the time, Pallas kernels for 0%

commit v1 on v0

v1 whole, which is shorter than its diff:
```python
import functools

import jax
import jax.numpy as jnp
from jax import lax
from jax.experimental import pallas as pl
from jax.experimental.pallas import tpu as pltpu
from jax.sharding import PartitionSpec as P

STEPS = 3
HALO = STEPS
WINDOW = 2 * HALO
GROUPS = ((0, 2), (2, 3), (3, 5))
VMEM_LIMIT = 48 * 1024 * 1024


def call(kernel, **kwargs):
    return pl.pallas_call(
        kernel,
        compiler_params=pltpu.CompilerParams(vmem_limit_bytes=VMEM_LIMIT),
        **kwargs,
    )


SMEM = pl.BlockSpec(memory_space=pltpu.SMEM)
VMEM = pl.BlockSpec(memory_space=pltpu.VMEM)


def to_neighbours(low_edge, high_edge, axis):
    count = lax.axis_size(axis)
    forward = [(i, i + 1) for i in range(count - 1)]
    backward = [(i + 1, i) for i in range(count - 1)]
    return lax.ppermute(high_edge, axis, forward), lax.ppermute(low_edge, axis, backward)


def ring_halo(below, above):
    gap = jnp.zeros(above.shape[:-2] + (8 - 2 * HALO, above.shape[-1]), above.dtype)
    return jnp.concatenate([above, gap, below], axis=-2)


def pack_kernel(sec_ref, x_ref, surface_ref, o_ref):
    step = pl.program_id(0)
    kinds, quarters, chunk, rows, lanes = x_ref.shape
    base = jnp.where(sec_ref[0] == 0, 128 - (128 - HALO), HALO)
    first = jnp.where(sec_ref[0] == 0, 0, HALO)
    lane = lax.broadcasted_iota(jnp.int32, (rows, lanes), 1)

    def placed(block, slot, total):
        at = 32 * slot[0] + WINDOW * slot[1]
        moved = pltpu.roll(block, lax.rem(base + at, 128), 1)
        inside = (lane >= at + first) & (lane < at + first + HALO)
        return jnp.where(inside, moved, total)

    def body(i, carry):
        total = jnp.zeros((rows, lanes), jnp.float32)
        for q in range(quarters):
            for v in range(kinds):
                total = placed(x_ref[v, q, i], (q, v), total)
        o_ref[step * chunk + i] = total
        return carry

    lax.fori_loop(0, chunk, body, 0, unroll=4)

    @pl.when(step == 0)
    def _():
        total = jnp.zeros((rows, lanes), jnp.float32)
        for q in range(2):
            for v in range(kinds):
                total = placed(surface_ref[q, v], (q, v), total)
        o_ref[o_ref.shape[0] - 1] = total


def window_kernel(own_ref, other_ref, own_halo_ref, other_halo_ref, coef_ref, mask_ref, h_ref):
    depth = h_ref.shape[1]
    rows = own_ref.shape[1]
    h_ref[0, :, :rows] = own_ref[:depth] + other_ref[:depth]
    h_ref[0, :, rows:] = own_halo_ref[:depth] + other_halo_ref[:depth]
    surface = jnp.concatenate(
        [
            own_ref[depth] + other_ref[depth],
            own_halo_ref[depth] + other_halo_ref[depth],
        ],
        axis=0,
    )
    lane = lax.broadcasted_iota(jnp.int32, surface.shape, 1)
    bottom = lane >= 96
    add_const = jnp.where(bottom, pltpu.roll(surface, 96, 1), 0.0)
    add_slope = jnp.where(bottom, pltpu.roll(surface, 64, 1), 0.0)
    ring = surface.shape[0]
    for s in range(STEPS - 1):

        def update(kk, above, below):
            f = h_ref[s, kk]
            c = [coef_ref[kk, pl.ds(n, 1), :] for n in range(6)]
            new = (
                c[0] * f
                + c[1] * pltpu.roll(f, 127, 1)
                + c[2] * pltpu.roll(f, 1, 1)
                + c[3] * pltpu.roll(f, ring - 1, 0)
                + c[4] * pltpu.roll(f, 1, 0)
                + c[5] * (above + below)
            )
            return f, new

        def store(kk, new):
            h_ref[s + 1, kk] = new * mask_ref[...]

        top, last = h_ref[s, 0], h_ref[s, depth - 1]
        _, new = update(0, jnp.where(lane < 32, top, pltpu.roll(last, 32, 1)), h_ref[s, 1])
        store(0, new)

        def body(kk, carry):
            _, new = update(kk, h_ref[s, kk - 1], h_ref[s, kk + 1])
            store(kk, new)
            return carry

        lax.fori_loop(1, depth - 1, body, 0, unroll=True)
        f, new = update(
            depth - 1, h_ref[s, depth - 2], jnp.where(bottom, last, pltpu.roll(top, 96, 1))
        )
        store(depth - 1, new + (add_const - add_slope * f))


def march_kernel(
    with_flux, first_kind, sec_ref, x_ref, halo_ref, surface_ref, surface_halo_ref, h_ref,
    coef_ref, mask_ref, *rest
):
    if with_flux:
        out_ref, flux_ref, s0, s1 = rest
    else:
        _, out_ref, s0, s1 = rest
    kind = pl.program_id(0) + first_kind
    levels, rows = x_ref.shape[1:3]
    quarter = levels // 4
    ring = s0.shape[1]
    s0[:, :rows] = x_ref[0]
    s0[:, rows:] = halo_ref[0]
    is_west = sec_ref[0] == 0
    source = jnp.where(is_west, HALO, HALO - 1) + WINDOW * kind
    goal = jnp.where(is_west, 127, 0)
    halo_mask = mask_ref[pl.ds(rows, ring - rows), :]
    flux = None
    states = (s0, s1, s0)
    for s in range(STEPS):
        src = states[s]
        for q in range(4):
            shift = lax.rem(goal + 256 - source - 32 * q, 128)

            def body(kk, carry, src=src, q=q, shift=shift, s=s):
                k = q * quarter + kk
                f = src[k]
                above = src[jnp.maximum(k - 1, 0)]
                below = src[jnp.minimum(k + 1, levels - 1)]
                c = [coef_ref[k, pl.ds(n, 1), :] for n in range(7)]
                north = pltpu.roll(f, ring - 1, 0)
                south = pltpu.roll(f, 1, 0)
                beside = h_ref[s, kk]
                if s == STEPS - 1:
                    f, above, below, north, south, beside = (
                        a[:rows] for a in (f, above, below, north, south, beside)
                    )
                new = (
                    c[0] * f
                    + c[1] * pltpu.roll(f, 127, 1)
                    + c[2] * pltpu.roll(f, 1, 1)
                    + c[6] * pltpu.roll(beside, shift, 1)
                    + c[3] * north
                    + c[4] * south
                    + c[5] * (above + below)
                )
                if s == STEPS - 1:
                    out_ref[0, k] = new
                else:
                    dst = states[s + 1]
                    dst[k, pl.ds(0, rows), :] = new[:rows]
                    dst[k, pl.ds(rows, ring - rows), :] = new[rows:] * halo_mask
                return carry

            lax.fori_loop(0, quarter, body, 0, unroll=True)
        last = src[levels - 1]
        term = surface_ref[0, 0] - surface_ref[1, 0] * last[:rows]
        if s == STEPS - 1:
            out_ref[0, levels - 1] += term
        else:
            dst = states[s + 1]
            dst[levels - 1, pl.ds(0, rows), :] += term
            dst[levels - 1, pl.ds(rows, ring - rows), :] += halo_mask * (
                surface_halo_ref[0, 0] - surface_halo_ref[1, 0] * last[rows:]
            )
        flux = term if flux is None else flux + term
    if with_flux:
        flux_ref[0] = flux


def march(group, sec, fields, halo, surface, surface_halo, seam, coef, mask, written):
    start, stop = group
    kinds, levels, rows, lanes = fields.shape
    with_flux = written is None
    ring = rows + 8
    in_specs = [
        SMEM,
        pl.BlockSpec((1, levels, rows, lanes), lambda v: (v + start, 0, 0, 0)),
        pl.BlockSpec((1, levels, 8, lanes), lambda v: (v + start, 0, 0, 0)),
        pl.BlockSpec((2, 1, rows, lanes), lambda v: (0, v + start, 0, 0)),
        pl.BlockSpec((2, 1, 8, lanes), lambda v: (0, v + start, 0, 0)),
        VMEM,
        VMEM,
        VMEM,
    ]
    operands = [sec, fields, halo, surface, surface_halo, seam, coef, mask]
    out_specs = [pl.BlockSpec((1, levels, rows, lanes), lambda v: (v + start, 0, 0, 0))]
    out_shape = [jax.ShapeDtypeStruct(fields.shape, jnp.float32)]
    aliases = {}
    if with_flux:
        out_specs.append(pl.BlockSpec((1, rows, lanes), lambda v: (v, 0, 0)))
        out_shape.append(jax.ShapeDtypeStruct((stop - start, rows, lanes), jnp.float32))
    else:
        in_specs.append(pl.BlockSpec(memory_space=pl.ANY))
        operands.append(written)
        aliases = {len(operands) - 1: 0}
    count = (stop - start) * levels * rows * lanes
    return pl.pallas_call(
        functools.partial(march_kernel, with_flux, start),
        grid=(stop - start,),
        in_specs=in_specs,
        out_specs=out_specs,
        out_shape=out_shape,
        scratch_shapes=[pltpu.VMEM((levels, ring, lanes), jnp.float32)] * 2,
        input_output_aliases=aliases,
        cost_estimate=pl.CostEstimate(
            flops=count * 60, bytes_accessed=count * 8, transcendentals=0
        ),
        compiler_params=pltpu.CompilerParams(vmem_limit_bytes=VMEM_LIMIT),
        name="march",
    )(*operands)


def column_kernel(mix_ref, x_ref, base_ref, first_ref, factor):
    levels = x_ref.shape[1]

    def mix(k):
        return jnp.full((1, 128), mix_ref[k], jnp.float32)

    def wide(row, width):
        return jnp.tile(row, (1, width // 128))

    width = x_ref.shape[2]
    inverse = 1.0 / (1.0 + mix(1))
    factor[pl.ds(0, 1), :] = mix(1) * inverse
    first_ref[pl.ds(0, 1), :] = inverse
    for v in range(2):
        base_ref[v, pl.ds(0, 1), :] = x_ref[v, pl.ds(0, 1), :] * wide(inverse, width)

    def forward(k, carry):
        scaled, ones, heat, salt = carry
        low = mix(k)
        inv = 1.0 / (1.0 + low + mix(k + 1) - low * scaled)
        new_scaled = mix(k + 1) * inv
        factor[pl.ds(k, 1), :] = new_scaled
        ones = ones * low * inv
        first_ref[pl.ds(k, 1), :] = ones
        low_w, inv_w = wide(low, width), wide(inv, width)
        heat = (x_ref[0, pl.ds(k, 1), :] + low_w * heat) * inv_w
        salt = (x_ref[1, pl.ds(k, 1), :] + low_w * salt) * inv_w
        base_ref[0, pl.ds(k, 1), :] = heat
        base_ref[1, pl.ds(k, 1), :] = salt
        return new_scaled, ones, heat, salt

    lax.fori_loop(
        1,
        levels,
        forward,
        (
            factor[pl.ds(0, 1), :],
            inverse,
            base_ref[0, pl.ds(0, 1), :],
            base_ref[1, pl.ds(0, 1), :],
        ),
    )

    def backward(i, carry):
        ones, heat, salt = carry
        k = levels - 2 - i
        c = factor[pl.ds(k, 1), :]
        c_w = wide(c, width)
        ones = first_ref[pl.ds(k, 1), :] + c * ones
        heat = base_ref[0, pl.ds(k, 1), :] + c_w * heat
        salt = base_ref[1, pl.ds(k, 1), :] + c_w * salt
        first_ref[pl.ds(k, 1), :] = ones
        base_ref[0, pl.ds(k, 1), :] = heat
        base_ref[1, pl.ds(k, 1), :] = salt
        return ones, heat, salt

    lax.fori_loop(
        0,
        levels - 1,
        backward,
        (
            first_ref[pl.ds(levels - 1, 1), :],
            base_ref[0, pl.ds(levels - 1, 1), :],
            base_ref[1, pl.ds(levels - 1, 1), :],
        ),
    )


def two_parts(x):
    high = x.astype(jnp.bfloat16)
    return high, (x - high.astype(jnp.float32)).astype(jnp.bfloat16)


def remap_kernel(
    extent_ref, low_ref, mid_ref, high_ref, site_ref, share_ref, base_ref, first_ref,
    solved_ref, contrib_ref
):
    columns = site_ref.shape[1]
    crossings = site_ref.shape[0]
    rows = mid_ref.shape[1]
    index = lax.broadcasted_iota(jnp.int32, (128, columns), 0)
    parts = []
    pad = jnp.zeros((128 - 3 * rows, 128), jnp.float32)
    for v in range(2):
        table = jnp.concatenate([low_ref[v], mid_ref[v], high_ref[v], pad], axis=0).T
        parts.append(jnp.concatenate(two_parts(table), axis=1))
    tables = jnp.concatenate(parts, axis=0)
    forcing = [jnp.zeros((1, columns), jnp.float32)] * 2
    picks = []
    for n in range(crossings):
        site = site_ref[pl.ds(n, 1), :]
        row, lane = lax.shift_right_logical(site, 7), site & 127
        hot = jnp.where(index == row, 1.0, 0.0).astype(jnp.bfloat16)
        picks.append((hot, index == lane))
        picked = jnp.dot(
            tables, jnp.concatenate([hot, hot], axis=0), preferred_element_type=jnp.float32
        )
        weight = jnp.where(index == lane, share_ref[pl.ds(n, 1), :], 0.0)
        for v in range(2):
            forcing[v] = forcing[v] + jnp.sum(
                picked[128 * v : 128 * (v + 1)] * weight, axis=0, keepdims=True
            )
    slot = lax.broadcasted_iota(jnp.int32, (1, columns), 1)
    live = jnp.where(slot < extent_ref[0], 1.0, 0.0)
    answer = jnp.tile(first_ref[...], (1, columns // 128))
    heat = (base_ref[0] - 0.5 * forcing[0] * answer) * live
    solved_ref[0] = heat
    solved_ref[1] = (base_ref[1] + 0.5 * forcing[1] * answer) * live
    top = heat[:1]
    total = jnp.zeros((128, 512), jnp.float32)
    for n in range(crossings):
        hot, at_lane = picks[n]
        weight = share_ref[pl.ds(n, 1), :] * live
        pieces = []
        for value in (weight * top, weight):
            high = value.astype(jnp.bfloat16).astype(jnp.float32)
            for part in (high, value - high):
                pieces.append(jnp.where(at_lane, part, 0.0).astype(jnp.bfloat16))
        total = total + lax.dot_general(
            hot,
            jnp.concatenate(pieces, axis=0),
            (((1,), (1,)), ((), ())),
            preferred_element_type=jnp.float32,
        )
    for v in range(2):
        both = total[:, 256 * v : 256 * v + 128] + total[:, 256 * v + 128 : 256 * v + 256]
        for part in range(3):
            contrib_ref[part, v] = both[part * rows : (part + 1) * rows]


def local(
    prognostic_quantities,
    advective_ratio,
    horizontal_diffuse_ratio,
    upright_diffuse_ratio,
    transfer_coefficient,
    terrain_outer_warmth,
    earlier_marine_warmth,
    marine_indicator,
    marine_salinity_heat_vector,
    marine_layer_diffuse_ratio,
    group_active_extent,
    intersect_air_site,
    intersect_interpolation_share,
):
    kinds, levels, rows, lanes = prognostic_quantities.shape
    ring = rows + 8
    quarter = levels // 4
    fields = prognostic_quantities
    tile_count = lax.axis_size("tile")
    sec_index, tile_index = lax.axis_index("sec"), lax.axis_index("tile")
    sec = sec_index.astype(jnp.int32).reshape(1)

    share = marine_indicator.astype(jnp.float32)
    outer = share * earlier_marine_warmth + (1.0 - share) * terrain_outer_warmth
    moist = transfer_coefficient * (0.3 + 0.7 * share)
    none = jnp.zeros_like(outer)
    surface = jnp.stack(
        [
            jnp.stack([transfer_coefficient * outer, moist * (0.6 * outer), none, none, none]),
            jnp.stack(
                [transfer_coefficient, moist, none, transfer_coefficient, transfer_coefficient]
            ),
        ]
    )

    def row_halo(block):
        below, above = to_neighbours(block[..., :HALO, :], block[..., -HALO:, :], "tile")
        return ring_halo(below, above)

    def with_surface(rows_of):
        terms = jnp.swapaxes(surface[:, :, rows_of], 0, 1)
        return jnp.concatenate([fields[:, :, rows_of], terms], axis=1)

    below, above = to_neighbours(
        with_surface(slice(0, HALO)), with_surface(slice(rows - HALO, rows)), "tile"
    )
    halo = ring_halo(below[:, :levels], above[:, :levels])
    surface_halo = jnp.swapaxes(ring_halo(below[:, levels:], above[:, levels:]), 0, 1)

    chunk = 8
    own = pl.pallas_call(
        pack_kernel,
        grid=(quarter // chunk,),
        in_specs=[
            SMEM,
            pl.BlockSpec((kinds, 4, chunk, rows, lanes), lambda i: (0, 0, i, 0, 0)),
            VMEM,
        ],
        out_specs=pl.BlockSpec((quarter + 1, rows, lanes), lambda i: (0, 0, 0)),
        out_shape=jax.ShapeDtypeStruct((quarter + 1, rows, lanes), jnp.float32),
        compiler_params=pltpu.CompilerParams(vmem_limit_bytes=VMEM_LIMIT),
        name="pack",
    )(sec, fields.reshape(kinds, 4, quarter, rows, lanes), surface)
    swap = [(0, 1), (1, 0)]
    other = lax.ppermute(own, "sec", swap)
    own_halo = row_halo(own)
    other_halo = lax.ppermute(own_halo, "sec", swap)

    h, u = horizontal_diffuse_ratio, upright_diffuse_ratio
    ax, ay = 0.5 * advective_ratio[0], 0.5 * advective_ratio[1]
    by_level = jnp.stack([1.0 - 4.0 * h - 2.0 * u, h - ax, h + ax, h - ay, h + ay, u, u, u], axis=1)
    lane = jnp.arange(lanes)
    east_edge, west_edge = lane == lanes - 1, lane == 0
    is_west = sec_index == 0
    wide = jnp.broadcast_to(by_level[:, :, None], (levels, 8, lanes))
    which = jnp.arange(8)[None, :, None]
    beside = jnp.where(is_west, (h - ax)[:, None] * east_edge, (h + ax)[:, None] * west_edge)
    coef = jnp.where((which == 1) & east_edge, 0.0, wide)
    coef = jnp.where((which == 2) & west_edge, 0.0, coef)
    coef = jnp.where(which == 6, beside[:, None, :], coef)
    window_coef = jnp.repeat(by_level.reshape(4, quarter, 8).transpose(1, 2, 0), 32, axis=2)
    row = jnp.arange(ring)
    inside = (
        (row < rows)
        | ((row < rows + HALO) & (tile_index < tile_count - 1))
        | ((row >= ring - HALO) & (tile_index > 0))
    )
    mask = jnp.broadcast_to(inside.astype(jnp.float32)[:, None], (ring, lanes))

    ocean_levels, columns = marine_salinity_heat_vector.shape[1:]
    mix = jnp.pad(marine_layer_diffuse_ratio, (1, 1))
    base, first = call(
        column_kernel,
        in_specs=[SMEM, VMEM],
        out_specs=[VMEM, VMEM],
        out_shape=[
            jax.ShapeDtypeStruct(marine_salinity_heat_vector.shape, jnp.float32),
            jax.ShapeDtypeStruct((ocean_levels, 128), jnp.float32),
        ],
        scratch_shapes=[pltpu.VMEM((ocean_levels, 128), jnp.float32)],
        name="columns",
    )(mix, marine_salinity_heat_vector)

    seam = call(
        window_kernel,
        in_specs=[VMEM] * 6,
        out_specs=VMEM,
        out_shape=jax.ShapeDtypeStruct((STEPS, quarter, ring, lanes), jnp.float32),
        name="seam",
    )(own, other, own_halo, other_halo, window_coef, mask)

    common = (surface, surface_halo, seam, coef, mask)
    tracers, flux = march(GROUPS[0], sec, fields, halo, *common, None)
    block_axes = ("sec", "tile")
    flux_low, flux_high = to_neighbours(flux, flux, block_axes)
    (tracers,) = march(GROUPS[1], sec, fields, halo, *common, tracers)
    resolved, contrib = call(
        remap_kernel,
        in_specs=[SMEM] + [VMEM] * 7,
        out_specs=[VMEM, VMEM],
        out_shape=[
            jax.ShapeDtypeStruct(marine_salinity_heat_vector.shape, jnp.float32),
            jax.ShapeDtypeStruct((3, 2, rows, lanes), jnp.float32),
        ],
        name="remap",
    )(
        group_active_extent,
        flux_low,
        flux,
        flux_high,
        intersect_air_site,
        intersect_interpolation_share,
        base,
        first,
    )
    from_low, from_high = to_neighbours(contrib[0], contrib[2], block_axes)
    (tracers,) = march(GROUPS[2], sec, fields, halo, *common, tracers)
    gathered = contrib[1] + from_low + from_high
    upcoming = (gathered[0] + earlier_marine_warmth) / (gathered[1] + 1.0)
    return (tracers, resolved, upcoming)


def solution(mesh):
    return jax.shard_map(
        local,
        mesh=mesh,
        in_specs=(
            P(None, None, "tile", "sec"),
            P(),
            P(),
            P(),
            P("tile", "sec"),
            P("tile", "sec"),
            P("tile", "sec"),
            P("tile", "sec"),
            P(None, None, ("sec", "tile")),
            P(),
            P(("sec", "tile")),
            P(None, ("sec", "tile")),
            P(None, ("sec", "tile")),
        ),
        out_specs=(P(None, None, "tile", "sec"), P(None, None, ("sec", "tile")), P("tile", "sec")),
        check_vma=False,
    )
```

time: 542 us -> 111 us (0.20)
  the two profiles are of different devices: /device:TPU:0 before, /device:TPU:29 now
where the time goes in v1:
time: 111 us; the launch traced here: 110 us
  Pallas kernels  53.2 us (48%)
  starting transfers between devices  30.1 us (27%)
  local copies, waits for them, and re-layouts  12.8 us (12%)
  waiting for transfers between devices  6.99 us (6%)
  other arithmetic  5.51 us (5%)
  between operations  1.73 us (2%)
    pallas_call x3, Pallas kernels, march(): pl.pallas_call(functools.partial(march_kernel, with_flux, start), grid=(s...  40 us
    ppermute x4, starting transfers between devices, to_neighbours(): lax.ppermute(low_edge, axis, backward)  17.6 us
    ppermute x4, starting transfers between devices, to_neighbours(): lax.ppermute(high_edge, axis, forward)  11 us
    ppermute x1, waiting for transfers between devices, local(): other_halo = lax.ppermute(own_halo, 'sec', swap)  6.96 us
    pallas_call x1, Pallas kernels, local(): pl.pallas_call(pack_kernel, grid=(quarter // chunk,), in_specs=[SMEM, pl....  6.29 us
    pallas_call x1, Pallas kernels, local(): call(column_kernel, in_specs=[SMEM, VMEM], out_specs=[VMEM, VMEM], out_sh...  3.32 us
    unnamed x32, local copies, waits for them, and re-layouts  3.12 us
    slice x1, local copies, waits for them, and re-layouts, with_surface(): return jnp.concatenate([fields[:, :, rows_of], terms], axis=1)  3 us
  transfers between devices with their start and end apart: 10, of which 1 were waited for; matrix products, arithmetic and copies ran while one was open for 5% of the time, Pallas kernels for 32%

profile of v1, /device:TPU:29, one launch (start us, length us, event | category | flops | bytes accessed | tf_op | source)
XLA Modules:
  0.0 110.3 jit_solution(11179919133950552447)
XLA Ops:
  0.6 0.7 constant_dynamic-update-slice_fusion.4
  1.4 0.7 constant_dynamic-update-slice_fusion.3
  2.1 0.7 constant_dynamic-update-slice_fusion.1
  2.8 0.7 constant_dynamic-update-slice_fusion
  3.5 0.8 multiply_bitcast_fusion.1
  4.3 0.1 pad.23.clone
  4.4 0.1 maximum_bitcast_fusion
  4.5 3.0 %fusion.10 = (f32[5,128,3,128]{3,2,1,0:T(4,128)S(1)}, f32[5,128,3,128]{3,2,1,0:T(4,128)S(1)}) fusion(f32[5,128,32,128]{3,2,1,0:T(8,128)} %x_ref.6), kind=kLoop, calls=%fused_computation.60 | loop fusion | bytes 3932160 | tf_op jit(solution)/shard_map/slice | solution.py:410
  7.5 0.1 copy.37
  7.6 1.0 pad_maximum_fusion.2
  8.7 1.3 %collective-permute-start.1 = (f32[5,130,3,128]{3,1,2,0:T(8,128)}, f32[5,130,3,128]{3,1,2,0:T(8,128)}, u32[]{:S(2)}, u32[]{:S(2)}) collective-permute-start(f32[5,130,3,128]{3,1,2,0:T(8,128)} %pad_maximum_fusion.2), channel_id=1, source_target_pairs={{0,1},{1,2},{2,3},{3,4},{4,5},{5,6},{6,7},{7,8},{8,9},{9,10},{10,1... | collective-permute-start | bytes 2995208 | tf_op jit(solution)/shard_map/ppermute | solution.py:33
  10.0 0.1 copy.35
  10.1 1.1 pad_maximum_fusion.1
  11.2 4.2 %collective-permute-start = (f32[5,130,3,128]{3,1,2,0:T(8,128)}, f32[5,130,3,128]{3,1,2,0:T(8,128)}, u32[]{:S(2)}, u32[]{:S(2)}) collective-permute-start(f32[5,130,3,128]{3,1,2,0:T(8,128)} %pad_maximum_fusion.1), channel_id=1, source_target_pairs={{1,0},{2,1},{3,2},{4,3},{5,4},{6,5},{7,6},{8,7},{9,8},{10,9},{11,1... | collective-permute-start | bytes 2995208 | tf_op jit(solution)/shard_map/ppermute | solution.py:33
  15.3 0.0 copy-start.4
  15.4 0.0 copy-start.5
  15.4 0.0 copy-start.6
  15.4 6.3 %pack.1.own_ref = f32[33,32,128]{2,1,0:T(8,128)S(1)} custom-call(s32[1]{0:T(128)} %bitcast.sec_ref, f32[5,4,32,32,128]{4,3,2,1,0:T(8,128)} %bitcast.52, f32[2,5,32,128]{3,2,1,0:T(8,128)S(1)} %pad_maximum_fusion.3.surface_ref), custom_call_target="tpu_custom_call" | custom-call | tf_op jit(solution)/shard_map/pack/pallas_call | solution.py:419
  21.7 1.3 %collective-permute-start.2 = (f32[33,32,128]{2,1,0:T(8,128)S(1)}, f32[33,32,128]{2,1,0:T(8,128)S(1)}, u32[]{:S(2)}, u32[]{:S(2)}) collective-permute-start(f32[33,32,128]{2,1,0:T(8,128)S(1)} %pack.1.own_ref), channel_id=1, source_target_pairs={{0,16},{16,0},{1,17},{17,1},{2,18},{18,2},{3,19},{19,3},{4,20},{20... | collective-permute-start | bytes 1622024 | tf_op jit(solution)/shard_map/ppermute | solution.py:433
  23.0 1.3 %collective-permute-start.4 = (f32[33,3,128]{2,1,0:T(4,128)S(1)}, f32[33,3,128]{2,1,0:T(4,128)S(1)}, u32[]{:S(2)}, u32[]{:S(2)}) collective-permute-start(f32[33,3,128]{2,1,0:T(4,128)S(1)} %get-tuple-element.18), channel_id=1, source_target_pairs={{0,1},{1,2},{2,3},{3,4},{4,5},{5,6},{6,7},{7,8},{8,9},{9,10},{10,1... | collective-permute-start | bytes 152072 | tf_op jit(solution)/shard_map/ppermute | solution.py:33
  24.3 3.6 %collective-permute-start.3 = (f32[33,3,128]{2,1,0:T(4,128)S(1)}, f32[33,3,128]{2,1,0:T(4,128)S(1)}, u32[]{:S(2)}, u32[]{:S(2)}) collective-permute-start(f32[33,3,128]{2,1,0:T(4,128)S(1)} %get-tuple-element.17), channel_id=1, source_target_pairs={{1,0},{2,1},{3,2},{4,3},{5,4},{6,5},{7,6},{8,7},{9,8},{10,9},{11,1... | collective-permute-start | bytes 152072 | tf_op jit(solution)/shard_map/ppermute | solution.py:33
  28.0 0.1 stack.84
  28.1 0.1 stack.79
  28.2 0.1 stack.80
  28.2 0.1 stack.81
  28.3 0.1 stack.82
  28.4 0.1 stack.83
  28.5 0.1 copy.34
  28.7 0.1 multiply_select_fusion
  28.8 0.1 broadcast_and_fusion
  28.9 0.2 select_select_fusion.coef_ref
  29.1 0.1 pad.12.clone
  29.2 0.0 collective-permute-done.4
  29.2 0.1 pad_maximum_fusion.4.own_halo_ref
  29.3 0.3 collective-permute-start.5
  29.6 0.1 copy.33
  29.7 0.3 broadcast_in_dim.69
  30.1 0.3 reshape.198.coef_ref
  30.4 7.0 %collective-permute-done.5.other_halo_ref = f32[33,8,128]{2,1,0:T(8,128)S(1)} collective-permute-done((f32[33,8,128]{2,1,0:T(8,128)S(1)}, f32[33,8,128]{2,1,0:T(8,128)S(1)}, u32[]{:S(2)}, u32[]{:S(2)}) %collective-permute-start.5) | collective-permute-done | bytes 135200 | tf_op jit(solution)/shard_map/ppermute | solution.py:435
  37.3 0.0 collective-permute-done.2.other_ref
  37.3 0.1 broadcast_in_dim.70.mask_ref
  37.4 1.1 seam.1.h_ref
  38.5 0.0 collective-permute-done.1
  38.5 1.3 %slice.73 = f32[5,128,3,128]{3,1,2,0:T(8,128)S(1)} slice(f32[5,130,3,128]{3,1,2,0:T(8,128)} %collective-permute-done.1), slice={[0:5], [0:128], [0:3], [0:128]} | slice | bytes 1966080 | tf_op jit(solution)/shard_map/slice | solution.py:415
  39.8 0.7 copy.38
  40.5 0.0 collective-permute-done
  40.5 1.3 %slice.70 = f32[5,128,3,128]{3,1,2,0:T(8,128)S(1)} slice(f32[5,130,3,128]{3,1,2,0:T(8,128)} %collective-permute-done), slice={[0:5], [0:128], [0:3], [0:128]} | slice | bytes 1966080 | tf_op jit(solution)/shard_map/slice | solution.py:415
  41.8 0.7 copy.36
  42.4 0.8 slice.75
  43.3 0.8 slice.74
  44.1 0.6 pad_maximum_fusion.halo_ref
  44.7 0.1 maximum_bitcast_fusion.1.surface_halo_ref
  44.8 0.0 copy-start.2
  44.8 15.5 %march.3 = (f32[5,128,32,128]{3,2,1,0:T(8,128)}, f32[2,32,128]{2,1,0:T(8,128)S(1)}) custom-call(s32[1]{0:T(128)} %bitcast.sec_ref, f32[5,128,32,128]{3,2,1,0:T(8,128)} %x_ref.6, f32[5,128,8,128]{3,2,1,0:T(8,128)S(1)} %pad_maximum_fusion.halo_ref, f32[2,5,32,128]{3,2,1,0:T(8,128)S(1)} %pad_maximum_fusion.3.surface_ref, ...), custom_call_target="tpu_custom_call" | custom-call | flops 62914560 | bytes 8388608 | tf_op jit(solution)/shard_map/march/pallas_call | solution.py:222
  60.3 2.9 %collective-permute-start.6 = (f32[2,32,128]{2,1,0:T(8,128)S(1)}, f32[2,32,128]{2,1,0:T(8,128)S(1)}, u32[]{:S(2)}, u32[]{:S(2)}) collective-permute-start(f32[2,32,128]{2,1,0:T(8,128)S(1)} %get-tuple-element.10.mid_ref), channel_id=1, source_target_pairs={{0,1},{1,2},{2,3},{3,4},{4,5},{5,6},{6,7},{7,8},{8,9},{9,10},{10,1... | collective-permute-start | bytes 98312 | tf_op jit(solution)/shard_map/ppermute | solution.py:33
  63.2 6.2 %collective-permute-start.7 = (f32[2,32,128]{2,1,0:T(8,128)S(1)}, f32[2,32,128]{2,1,0:T(8,128)S(1)}, u32[]{:S(2)}, u32[]{:S(2)}) collective-permute-start(f32[2,32,128]{2,1,0:T(8,128)S(1)} %get-tuple-element.10.mid_ref), channel_id=1, source_target_pairs={{1,0},{2,1},{3,2},{4,3},{5,4},{6,5},{7,6},{8,7},{9,8},{10,9},{11,1... | collective-permute-start | bytes 98312 | tf_op jit(solution)/shard_map/ppermute | solution.py:33
  70.0 0.1 pad.4.mix_ref
  70.1 3.3 %columns.1 = (f32[2,80,1024]{2,1,0:T(8,128)S(1)}, f32[80,128]{1,0:T(8,128)S(1)}) custom-call(f32[81]{0:T(128)S(1)} %pad.4.mix_ref, f32[2,80,1024]{2,1,0:T(8,128)S(1)} %copy-done), custom_call_target="tpu_custom_call" | custom-call | tf_op jit(solution)/shard_map/columns/pallas_call | solution.py:460
  73.4 2.4 %remap.1 = (f32[2,80,1024]{2,1,0:T(8,128)}, f32[3,2,32,128]{3,2,1,0:T(8,128)S(1)}) custom-call(s32[1]{0:T(128)S(6)} %copy.54.extent_ref, f32[2,32,128]{2,1,0:T(8,128)S(1)} %collective-permute-done.6.low_ref, f32[2,32,128]{2,1,0:T(8,128)S(1)} %get-tuple-element.10.mid_ref, f32[2,32,128]{2,1,0:T(8,128)S(1)} %collective-permute-done.7.high_ref, ...), custom_call_target="tpu_custom_call" | custom-call | tf_op jit(solution)/shard_map/remap/pallas_call | solution.py:485
  75.9 3.6 %collective-permute-start.9 = (f32[2,32,128]{2,1,0:T(8,128)S(1)}, f32[2,32,128]{2,1,0:T(8,128)S(1)}, u32[]{:S(2)}, u32[]{:S(2)}) collective-permute-start(f32[2,32,128]{2,1,0:T(8,128)S(1)} %get-tuple-element.22), channel_id=1, source_target_pairs={{1,0},{2,1},{3,2},{4,3},{5,4},{6,5},{7,6},{8,7},{9,8},{10,9},{11,1... | collective-permute-start | bytes 98312 | tf_op jit(solution)/shard_map/ppermute | solution.py:33
  79.5 5.5 %collective-permute-start.8 = (f32[2,32,128]{2,1,0:T(8,128)S(1)}, f32[2,32,128]{2,1,0:T(8,128)S(1)}, u32[]{:S(2)}, u32[]{:S(2)}) collective-permute-start(f32[2,32,128]{2,1,0:T(8,128)S(1)} %get-tuple-element.21), channel_id=1, source_target_pairs={{0,1},{1,2},{2,3},{3,4},{4,5},{5,6},{6,7},{7,8},{8,9},{9,10},{10,1... | collective-permute-start | bytes 98312 | tf_op jit(solution)/shard_map/ppermute | solution.py:33
  85.1 9.2 %march.4.rest_0_ = f32[5,128,32,128]{3,2,1,0:T(8,128)} custom-call(s32[1]{0:T(128)} %bitcast.sec_ref, f32[5,128,32,128]{3,2,1,0:T(8,128)} %x_ref.6, f32[5,128,8,128]{3,2,1,0:T(8,128)S(1)} %pad_maximum_fusion.halo_ref, f32[2,5,32,128]{3,2,1,0:T(8,128)S(1)} %pad_maximum_fusion.3.surface_ref, ...), custom_call_target="tpu_custom_call", output_to_operand_aliasing={{}: (8, {})} | custom-call | flops 31457280 | bytes 4194304 | tf_op jit(solution)/shard_map/march/pallas_call | solution.py:222
  94.2 15.4 %march.5 = f32[5,128,32,128]{3,2,1,0:T(8,128)} custom-call(s32[1]{0:T(128)} %bitcast.sec_ref, f32[5,128,32,128]{3,2,1,0:T(8,128)} %x_ref.6, f32[5,128,8,128]{3,2,1,0:T(8,128)S(1)} %pad_maximum_fusion.halo_ref, f32[2,5,32,128]{3,2,1,0:T(8,128)S(1)} %pad_maximum_fusion.3.surface_ref, ...), custom_call_target="tpu_custom_call", output_to_operand_aliasing={{}: (8, {})} | custom-call | flops 62914560 | bytes 8388608 | tf_op jit(solution)/shard_map/march/pallas_call | solution.py:222
  109.7 0.6 fusion.6
  (46 shorter events, 0.3 us)
Async XLA Ops:
  8.7 29.8 %collective-permute-start.1 = (f32[5,130,3,128]{3,1,2,0:T(8,128)}, f32[5,130,3,128]{3,1,2,0:T(8,128)}, u32[]{:S(2)}, u32[]{:S(2)}) collective-permute-start(f32[5,130,3,128]{3,1,2,0:T(8,128)} %pad_maximum_fusion.2), channel_id=1, source_target_pairs={{0,1},{1,2},{2,3},{3,4},{4,5},{5,6},{6,7},{7,8},{8,9},{9,10},{10,1... | collective-permute-start | bytes 2995208 | tf_op jit(solution)/shard_map/ppermute | solution.py:33
  11.2 29.3 %collective-permute-start = (f32[5,130,3,128]{3,1,2,0:T(8,128)}, f32[5,130,3,128]{3,1,2,0:T(8,128)}, u32[]{:S(2)}, u32[]{:S(2)}) collective-permute-start(f32[5,130,3,128]{3,1,2,0:T(8,128)} %pad_maximum_fusion.1), channel_id=1, source_target_pairs={{1,0},{2,1},{3,2},{4,3},{5,4},{6,5},{7,6},{8,7},{9,8},{10,9},{11,1... | collective-permute-start | bytes 2995208 | tf_op jit(solution)/shard_map/ppermute | solution.py:33
  15.3 12.6 %copy-start.4 = (f32[128]{0:T(128)S(1)}, f32[128]{0:T(128)}, u32[]{:S(2)}) copy-start(f32[128]{0:T(128)} %param.16) | copy-start | bytes 1540
  15.4 12.7 %copy-start.5 = (f32[2,128]{1,0:T(2,128)S(1)}, f32[2,128]{1,0:T(2,128)}, u32[]{:S(2)}) copy-start(f32[2,128]{1,0:T(2,128)} %param.14) | copy-start | bytes 3076
  15.4 12.7 %copy-start.6 = (f32[128]{0:T(128)S(1)}, f32[128]{0:T(128)}, u32[]{:S(2)}) copy-start(f32[128]{0:T(128)} %param.15) | copy-start | bytes 1540
  21.7 15.6 %collective-permute-start.2 = (f32[33,32,128]{2,1,0:T(8,128)S(1)}, f32[33,32,128]{2,1,0:T(8,128)S(1)}, u32[]{:S(2)}, u32[]{:S(2)}) collective-permute-start(f32[33,32,128]{2,1,0:T(8,128)S(1)} %pack.1.own_ref), channel_id=1, source_target_pairs={{0,16},{16,0},{1,17},{17,1},{2,18},{18,2},{3,19},{19,3},{4,20},{20... | collective-permute-start | bytes 1622024 | tf_op jit(solution)/shard_map/ppermute | solution.py:433
  23.0 6.2 %collective-permute-start.4 = (f32[33,3,128]{2,1,0:T(4,128)S(1)}, f32[33,3,128]{2,1,0:T(4,128)S(1)}, u32[]{:S(2)}, u32[]{:S(2)}) collective-permute-start(f32[33,3,128]{2,1,0:T(4,128)S(1)} %get-tuple-element.18), channel_id=1, source_target_pairs={{0,1},{1,2},{2,3},{3,4},{4,5},{5,6},{6,7},{7,8},{8,9},{9,10},{10,1... | collective-permute-start | bytes 152072 | tf_op jit(solution)/shard_map/ppermute | solution.py:33
  24.3 4.9 %collective-permute-start.3 = (f32[33,3,128]{2,1,0:T(4,128)S(1)}, f32[33,3,128]{2,1,0:T(4,128)S(1)}, u32[]{:S(2)}, u32[]{:S(2)}) collective-permute-start(f32[33,3,128]{2,1,0:T(4,128)S(1)} %get-tuple-element.17), channel_id=1, source_target_pairs={{1,0},{2,1},{3,2},{4,3},{5,4},{6,5},{7,6},{8,7},{9,8},{10,9},{11,1... | collective-permute-start | bytes 152072 | tf_op jit(solution)/shard_map/ppermute | solution.py:33
  29.3 8.1 %collective-permute-start.5 = (f32[33,8,128]{2,1,0:T(8,128)S(1)}, f32[33,8,128]{2,1,0:T(8,128)S(1)}, u32[]{:S(2)}, u32[]{:S(2)}) collective-permute-start(f32[33,8,128]{2,1,0:T(8,128)S(1)} %pad_maximum_fusion.4.own_halo_ref), channel_id=1, source_target_pairs={{0,16},{16,0},{1,17},{17,1},{2,18},{18,2},{3,19},{19,3},{4,20},{20... | collective-permute-start | bytes 405512 | tf_op jit(solution)/shard_map/ppermute | solution.py:435
  44.8 25.2 %copy-start.7 = (f32[79]{0:T(128)S(1)}, f32[79]{0:T(128)}, u32[]{:S(2)}) copy-start(f32[79]{0:T(128)} %param.22) | copy-start | bytes 952
  44.8 25.3 %copy-start = (f32[2,80,1024]{2,1,0:T(8,128)S(1)}, f32[2,80,1024]{2,1,0:T(8,128)}, u32[]{:S(2)}) copy-start(f32[2,80,1024]{2,1,0:T(8,128)} %x_ref.7) | copy-start | bytes 1966084
  44.8 28.6 %copy-start.1 = (s32[4,1024]{1,0:T(4,128)S(1)}, s32[4,1024]{1,0:T(4,128)}, u32[]{:S(2)}) copy-start(s32[4,1024]{1,0:T(4,128)} %site_ref.1) | copy-start | bytes 49156
  44.8 28.6 %copy-start.2 = (f32[4,1024]{1,0:T(4,128)S(1)}, f32[4,1024]{1,0:T(4,128)}, u32[]{:S(2)}) copy-start(f32[4,1024]{1,0:T(4,128)} %share_ref.1) | copy-start | bytes 49156
  60.3 13.1 %collective-permute-start.6 = (f32[2,32,128]{2,1,0:T(8,128)S(1)}, f32[2,32,128]{2,1,0:T(8,128)S(1)}, u32[]{:S(2)}, u32[]{:S(2)}) collective-permute-start(f32[2,32,128]{2,1,0:T(8,128)S(1)} %get-tuple-element.10.mid_ref), channel_id=1, source_target_pairs={{0,1},{1,2},{2,3},{3,4},{4,5},{5,6},{6,7},{7,8},{8,9},{9,10},{10,1... | collective-permute-start | bytes 98312 | tf_op jit(solution)/shard_map/ppermute | solution.py:33
  63.2 10.2 %collective-permute-start.7 = (f32[2,32,128]{2,1,0:T(8,128)S(1)}, f32[2,32,128]{2,1,0:T(8,128)S(1)}, u32[]{:S(2)}, u32[]{:S(2)}) collective-permute-start(f32[2,32,128]{2,1,0:T(8,128)S(1)} %get-tuple-element.10.mid_ref), channel_id=1, source_target_pairs={{1,0},{2,1},{3,2},{4,3},{5,4},{6,5},{7,6},{8,7},{9,8},{10,9},{11,1... | collective-permute-start | bytes 98312 | tf_op jit(solution)/shard_map/ppermute | solution.py:33
  75.9 33.7 %collective-permute-start.9 = (f32[2,32,128]{2,1,0:T(8,128)S(1)}, f32[2,32,128]{2,1,0:T(8,128)S(1)}, u32[]{:S(2)}, u32[]{:S(2)}) collective-permute-start(f32[2,32,128]{2,1,0:T(8,128)S(1)} %get-tuple-element.22), channel_id=1, source_target_pairs={{1,0},{2,1},{3,2},{4,3},{5,4},{6,5},{7,6},{8,7},{9,8},{10,9},{11,1... | collective-permute-start | bytes 98312 | tf_op jit(solution)/shard_map/ppermute | solution.py:33
  79.5 30.1 %collective-permute-start.8 = (f32[2,32,128]{2,1,0:T(8,128)S(1)}, f32[2,32,128]{2,1,0:T(8,128)S(1)}, u32[]{:S(2)}, u32[]{:S(2)}) collective-permute-start(f32[2,32,128]{2,1,0:T(8,128)S(1)} %get-tuple-element.21), channel_id=1, source_target_pairs={{0,1},{1,2},{2,3},{3,4},{4,5},{5,6},{6,7},{7,8},{8,9},{9,10},{10,1... | collective-permute-start | bytes 98312 | tf_op jit(solution)/shard_map/ppermute | solution.py:33
  94.2 15.4 %copy-start.3 = (f32[32,128]{1,0:T(8,128)S(1)}, f32[32,128]{1,0:T(8,128)}, u32[]{:S(2)}) copy-start(f32[32,128]{1,0:T(8,128)} %param.19) | copy-start | bytes 49156

commit v2 on v1

--- a/solution.py
+++ b/solution.py
@@ -1,5 +1,3 @@
-import functools
-
 import jax
 import jax.numpy as jnp
 from jax import lax
@@ -10,7 +8,6 @@
 STEPS = 3
 HALO = STEPS
 WINDOW = 2 * HALO
-GROUPS = ((0, 2), (2, 3), (3, 5))
 VMEM_LIMIT = 48 * 1024 * 1024
 
 
@@ -122,19 +119,14 @@
 
 
 def march_kernel(
-    with_flux, first_kind, sec_ref, x_ref, halo_ref, surface_ref, surface_halo_ref, h_ref,
-    coef_ref, mask_ref, *rest
+    sec_ref, x_ref, halo_ref, surface_ref, h_ref, coef_ref, mask_ref, out_ref, flux_ref, s0, s1
 ):
-    if with_flux:
-        out_ref, flux_ref, s0, s1 = rest
-    else:
-        _, out_ref, s0, s1 = rest
-    kind = pl.program_id(0) + first_kind
+    kind = pl.program_id(0)
     levels, rows = x_ref.shape[1:3]
     quarter = levels // 4
     ring = s0.shape[1]
     s0[:, :rows] = x_ref[0]
-    s0[:, rows:] = halo_ref[0]
+    s0[:, rows:] = halo_ref[0, :levels]
     is_west = sec_ref[0] == 0
     source = jnp.where(is_west, HALO, HALO - 1) + WINDOW * kind
     goal = jnp.where(is_west, 127, 0)
@@ -185,54 +177,39 @@
             dst = states[s + 1]
             dst[levels - 1, pl.ds(0, rows), :] += term
             dst[levels - 1, pl.ds(rows, ring - rows), :] += halo_mask * (
-                surface_halo_ref[0, 0] - surface_halo_ref[1, 0] * last[rows:]
+                halo_ref[0, levels] - halo_ref[0, levels + 1] * last[rows:]
             )
         flux = term if flux is None else flux + term
-    if with_flux:
-        flux_ref[0] = flux
-
-
-def march(group, sec, fields, halo, surface, surface_halo, seam, coef, mask, written):
-    start, stop = group
+    flux_ref[0] = flux
+
+
+def march(sec, fields, halo, surface, seam, coef, mask):
     kinds, levels, rows, lanes = fields.shape
-    with_flux = written is None
-    ring = rows + 8
-    in_specs = [
-        SMEM,
-        pl.BlockSpec((1, levels, rows, lanes), lambda v: (v + start, 0, 0, 0)),
-        pl.BlockSpec((1, levels, 8, lanes), lambda v: (v + start, 0, 0, 0)),
-        pl.BlockSpec((2, 1, rows, lanes), lambda v: (0, v + start, 0, 0)),
-        pl.BlockSpec((2, 1, 8, lanes), lambda v: (0, v + start, 0, 0)),
-        VMEM,
-        VMEM,
-        VMEM,
-    ]
-    operands = [sec, fields, halo, surface, surface_halo, seam, coef, mask]
-    out_specs = [pl.BlockSpec((1, levels, rows, lanes), lambda v: (v + start, 0, 0, 0))]
-    out_shape = [jax.ShapeDtypeStruct(fields.shape, jnp.float32)]
-    aliases = {}
-    if with_flux:
-        out_specs.append(pl.BlockSpec((1, rows, lanes), lambda v: (v, 0, 0)))
-        out_shape.append(jax.ShapeDtypeStruct((stop - start, rows, lanes), jnp.float32))
-    else:
-        in_specs.append(pl.BlockSpec(memory_space=pl.ANY))
-        operands.append(written)
-        aliases = {len(operands) - 1: 0}
-    count = (stop - start) * levels * rows * lanes
+    block = pl.BlockSpec((1, levels, rows, lanes), lambda v: (v, 0, 0, 0))
     return pl.pallas_call(
-        functools.partial(march_kernel, with_flux, start),
-        grid=(stop - start,),
-        in_specs=in_specs,
-        out_specs=out_specs,
-        out_shape=out_shape,
-        scratch_shapes=[pltpu.VMEM((levels, ring, lanes), jnp.float32)] * 2,
-        input_output_aliases=aliases,
+        march_kernel,
+        grid=(kinds,),
+        in_specs=[
+            SMEM,
+            block,
+            pl.BlockSpec((1, levels + 2, 8, lanes), lambda v: (v, 0, 0, 0)),
+            pl.BlockSpec((2, 1, rows, lanes), lambda v: (0, v, 0, 0)),
+            VMEM,
+            VMEM,
+            VMEM,
+        ],
+        out_specs=[block, pl.BlockSpec((1, rows, lanes), lambda v: (v, 0, 0))],
+        out_shape=[
+            jax.ShapeDtypeStruct(fields.shape, jnp.float32),
+            jax.ShapeDtypeStruct((kinds, rows, lanes), jnp.float32),
+        ],
+        scratch_shapes=[pltpu.VMEM((levels, rows + 8, lanes), jnp.float32)] * 2,
         cost_estimate=pl.CostEstimate(
-            flops=count * 60, bytes_accessed=count * 8, transcendentals=0
+            flops=fields.size * 60, bytes_accessed=fields.size * 8, transcendentals=0
         ),
         compiler_params=pltpu.CompilerParams(vmem_limit_bytes=VMEM_LIMIT),
         name="march",
-    )(*operands)
+    )(sec, fields, halo, surface, seam, coef, mask)
 
 
 def column_kernel(mix_ref, x_ref, base_ref, first_ref, factor):
@@ -308,18 +285,50 @@
     return high, (x - high.astype(jnp.float32)).astype(jnp.bfloat16)
 
 
+def exchange(sources, landing, send_sem, recv_sem, first, below, above):
+    copies = []
+    for n, device in enumerate((below, above)):
+        copy = pltpu.make_async_remote_copy(
+            src_ref=sources[n],
+            dst_ref=landing.at[1 - n],
+            send_sem=send_sem.at[first + n],
+            recv_sem=recv_sem.at[first + 1 - n],
+            device_id=device,
+            device_id_type=pl.DeviceIdType.MESH,
+        )
+        copy.start()
+        copies.append(copy)
+    return copies
+
+
 def remap_kernel(
-    extent_ref, low_ref, mid_ref, high_ref, site_ref, share_ref, base_ref, first_ref,
-    solved_ref, contrib_ref
+    extent_ref, flux_ref, site_ref, share_ref, base_ref, first_ref, earlier_ref,
+    solved_ref, warmth_ref, landed, outgoing, arrived, send_sem, recv_sem
 ):
+    tiles = lax.axis_size("tile")
+    blocks = tiles * lax.axis_size("sec")
+    block = lax.axis_index("sec") * tiles + lax.axis_index("tile")
+    near = []
+    for away in (blocks - 1, 1):
+        other = lax.rem(block + away, blocks)
+        near.append((lax.div(other, tiles), lax.rem(other, tiles)))
+    barrier = pltpu.get_barrier_semaphore()
+    for device in near:
+        pl.semaphore_signal(
+            barrier, inc=1, device_id=device, device_id_type=pl.DeviceIdType.MESH
+        )
+    pl.semaphore_wait(barrier, 2)
+    own = flux_ref.at[pl.ds(0, 2)]
+    for copy in exchange((own, own), landed, send_sem, recv_sem, 0, *near):
+        copy.wait()
     columns = site_ref.shape[1]
     crossings = site_ref.shape[0]
-    rows = mid_ref.shape[1]
+    rows = flux_ref.shape[1]
     index = lax.broadcasted_iota(jnp.int32, (128, columns), 0)
     parts = []
     pad = jnp.zeros((128 - 3 * rows, 128), jnp.float32)
     for v in range(2):
-        table = jnp.concatenate([low_ref[v], mid_ref[v], high_ref[v], pad], axis=0).T
+        table = jnp.concatenate([landed[0, v], flux_ref[v], landed[1, v], pad], axis=0).T
         parts.append(jnp.concatenate(two_parts(table), axis=1))
     tables = jnp.concatenate(parts, axis=0)
     forcing = [jnp.zeros((1, columns), jnp.float32)] * 2
@@ -359,10 +368,17 @@
             (((1,), (1,)), ((), ())),
             preferred_element_type=jnp.float32,
         )
+    mine = []
     for v in range(2):
         both = total[:, 256 * v : 256 * v + 128] + total[:, 256 * v + 128 : 256 * v + 256]
-        for part in range(3):
-            contrib_ref[part, v] = both[part * rows : (part + 1) * rows]
+        outgoing[0, v] = both[:rows]
+        mine.append(both[rows : 2 * rows])
+        outgoing[1, v] = both[2 * rows : 3 * rows]
+    sources = (outgoing.at[0], outgoing.at[1])
+    for copy in exchange(sources, arrived, send_sem, recv_sem, 2, *near):
+        copy.wait()
+    heat_in, weight_in = (mine[v] + arrived[0, v] + arrived[1, v] for v in range(2))
+    warmth_ref[...] = (heat_in + earlier_ref[...]) / (weight_in + 1.0)
 
 
 def local(
@@ -412,8 +428,7 @@
     below, above = to_neighbours(
         with_surface(slice(0, HALO)), with_surface(slice(rows - HALO, rows)), "tile"
     )
-    halo = ring_halo(below[:, :levels], above[:, :levels])
-    surface_halo = jnp.swapaxes(ring_halo(below[:, levels:], above[:, levels:]), 0, 1)
+    halo = ring_halo(below, above)
 
     chunk = 8
     own = pl.pallas_call(
@@ -477,34 +492,31 @@
         name="seam",
     )(own, other, own_halo, other_halo, window_coef, mask)
 
-    common = (surface, surface_halo, seam, coef, mask)
-    tracers, flux = march(GROUPS[0], sec, fields, halo, *common, None)
-    block_axes = ("sec", "tile")
-    flux_low, flux_high = to_neighbours(flux, flux, block_axes)
-    (tracers,) = march(GROUPS[1], sec, fields, halo, *common, tracers)
-    resolved, contrib = call(
+    tracers, flux = march(sec, fields, halo, surface, seam, coef, mask)
+    pair = (2, 2, rows, lanes)
+    resolved, upcoming = pl.pallas_call(
         remap_kernel,
-        in_specs=[SMEM] + [VMEM] * 7,
+        in_specs=[SMEM] + [VMEM] * 6,
         out_specs=[VMEM, VMEM],
         out_shape=[
             jax.ShapeDtypeStruct(marine_salinity_heat_vector.shape, jnp.float32),
-            jax.ShapeDtypeStruct((3, 2, rows, lanes), jnp.float32),
+            jax.ShapeDtypeStruct((rows, lanes), jnp.float32),
         ],
+        scratch_shapes=[pltpu.VMEM(pair, jnp.float32)] * 3
+        + [pltpu.SemaphoreType.DMA((4,)), pltpu.SemaphoreType.DMA((4,))],
+        compiler_params=pltpu.CompilerParams(
+            vmem_limit_bytes=VMEM_LIMIT, collective_id=0, has_side_effects=True
+        ),
         name="remap",
     )(
         group_active_extent,
-        flux_low,
         flux,
-        flux_high,
         intersect_air_site,
         intersect_interpolation_share,
         base,
         first,
-    )
-    from_low, from_high = to_neighbours(contrib[0], contrib[2], block_axes)
-    (tracers,) = march(GROUPS[2], sec, fields, halo, *common, tracers)
-    gathered = contrib[1] + from_low + from_high
-    upcoming = (gathered[0] + earlier_marine_warmth) / (gathered[1] + 1.0)
+        earlier_marine_warmth,
+    )
     return (tracers, resolved, upcoming)
 
 

time: 111 us -> 101 us (0.910)
  the two profiles are of different devices: /device:TPU:29 before, /device:TPU:0 now
where the time goes in v2:
time: 101 us; the launch traced here: 99.8 us
  Pallas kernels  66.8 us (66%)
  starting transfers between devices  14 us (14%)
  local copies, waits for them, and re-layouts  11.7 us (12%)
  other arithmetic  4.79 us (5%)
  between operations  1.62 us (2%)
    pallas_call x1, Pallas kernels, march(): pl.pallas_call(march_kernel, grid=(kinds,), in_specs=[SMEM, block, pl.Blo...  33.1 us
    pallas_call x1, Pallas kernels, local(): pl.pallas_call(remap_kernel, in_specs=[SMEM] + [VMEM] * 6, out_specs=[VME...  23.1 us
    ppermute x2, starting transfers between devices, to_neighbours(): lax.ppermute(high_edge, axis, forward)  7.7 us
    pallas_call x1, Pallas kernels, local(): pl.pallas_call(pack_kernel, grid=(quarter // chunk,), in_specs=[SMEM, pl....  6.29 us
    pallas_call x1, Pallas kernels, local(): call(column_kernel, in_specs=[SMEM, VMEM], out_specs=[VMEM, VMEM], out_sh...  3.32 us
    unnamed x30, local copies, waits for them, and re-layouts  3.19 us
    ppermute x1, starting transfers between devices, local(): other = lax.ppermute(own, 'sec', swap)  3 us
    slice x1, local copies, waits for them, and re-layouts, with_surface(): return jnp.concatenate([fields[:, :, rows_of], terms], axis=1)  3 us
  transfers between devices with their start and end apart: 6, of which 1 were waited for; matrix products, arithmetic and copies ran while one was open for 9% of the time, Pallas kernels for 4%

profile of v2, /device:TPU:0, one launch (start us, length us, event | category | flops | bytes accessed | tf_op | source)
XLA Modules:
  0.0 99.8 jit_solution(8980451248770401213)
XLA Ops:
  0.6 0.7 constant_dynamic-update-slice_fusion.4
  1.4 0.7 constant_dynamic-update-slice_fusion.3
  2.1 0.7 constant_dynamic-update-slice_fusion.1
  2.8 0.7 constant_dynamic-update-slice_fusion
  3.5 0.8 multiply_bitcast_fusion.1
  4.3 0.1 pad.20.clone
  4.4 0.1 maximum_bitcast_fusion
  4.5 6.3 %pack.1.own_ref = f32[33,32,128]{2,1,0:T(8,128)S(1)} custom-call(s32[1]{0:T(128)} %bitcast.sec_ref, f32[5,4,32,32,128]{4,3,2,1,0:T(8,128)} %bitcast.32, f32[2,5,32,128]{3,2,1,0:T(8,128)S(1)} %pad_maximum_fusion.3.surface_ref), custom_call_target="tpu_custom_call" | custom-call | tf_op jit(solution)/shard_map/pack/pallas_call | solution.py:434
  10.8 3.0 %collective-permute-start.2 = (f32[33,32,128]{2,1,0:T(8,128)S(1)}, f32[33,32,128]{2,1,0:T(8,128)S(1)}, u32[]{:S(2)}, u32[]{:S(2)}) collective-permute-start(f32[33,32,128]{2,1,0:T(8,128)S(1)} %pack.1.own_ref), channel_id=1, source_target_pairs={{0,16},{16,0},{1,17},{17,1},{2,18},{18,2},{3,19},{19,3},{4,20},{20... | collective-permute-start | bytes 1622024 | tf_op jit(solution)/shard_map/ppermute | solution.py:448
  13.8 1.3 %collective-permute-start.3 = (f32[33,3,128]{2,1,0:T(4,128)S(1)}, f32[33,3,128]{2,1,0:T(4,128)S(1)}, u32[]{:S(2)}, u32[]{:S(2)}) collective-permute-start(f32[33,3,128]{2,1,0:T(4,128)S(1)} %get-tuple-element.17), channel_id=1, source_target_pairs={{1,0},{2,1},{3,2},{4,3},{5,4},{6,5},{7,6},{8,7},{9,8},{10,9},{11,1... | collective-permute-start | bytes 152072 | tf_op jit(solution)/shard_map/ppermute | solution.py:30
  15.1 3.0 %collective-permute-start.4 = (f32[33,3,128]{2,1,0:T(4,128)S(1)}, f32[33,3,128]{2,1,0:T(4,128)S(1)}, u32[]{:S(2)}, u32[]{:S(2)}) collective-permute-start(f32[33,3,128]{2,1,0:T(4,128)S(1)} %get-tuple-element.18), channel_id=1, source_target_pairs={{0,1},{1,2},{2,3},{3,4},{4,5},{5,6},{6,7},{7,8},{8,9},{9,10},{10,1... | collective-permute-start | bytes 152072 | tf_op jit(solution)/shard_map/ppermute | solution.py:30
  18.2 3.0 %fusion.6 = (f32[5,128,3,128]{3,2,1,0:T(4,128)S(1)}, f32[5,128,3,128]{3,2,1,0:T(4,128)S(1)}) fusion(f32[5,128,32,128]{3,2,1,0:T(8,128)} %x_ref.2), kind=kLoop, calls=%fused_computation.50 | loop fusion | bytes 3932160 | tf_op jit(solution)/shard_map/slice | solution.py:426
  21.2 0.1 copy.28
  21.3 1.0 %pad_maximum_fusion.1 = f32[5,130,3,128]{3,1,2,0:T(8,128)} fusion(f32[5,2,3,128]{3,1,2,0:T(2,128)S(1)} %copy.21, f32[5,128,3,128]{3,1,2,0:T(8,128)S(1)} %copy.28), kind=kLoop, calls=%fused_computation.1 | loop fusion | flops 249600 | bytes 1996800 | tf_op jit(solution)/shard_map/concatenate | solution.py:426
  22.4 1.4 %collective-permute-start = (f32[5,130,3,128]{3,1,2,0:T(8,128)}, f32[5,130,3,128]{3,1,2,0:T(8,128)}, u32[]{:S(2)}, u32[]{:S(2)}) collective-permute-start(f32[5,130,3,128]{3,1,2,0:T(8,128)} %pad_maximum_fusion.1), channel_id=1, source_target_pairs={{1,0},{2,1},{3,2},{4,3},{5,4},{6,5},{7,6},{8,7},{9,8},{10,9},{11,1... | collective-permute-start | bytes 2995208 | tf_op jit(solution)/shard_map/ppermute | solution.py:30
  23.8 0.1 copy.29
  23.9 0.0 copy-start.7
  23.9 0.0 copy-start
  23.9 1.0 %pad_maximum_fusion.2 = f32[5,130,3,128]{3,1,2,0:T(8,128)} fusion(f32[5,2,3,128]{3,1,2,0:T(2,128)S(1)} %copy.23, f32[5,128,3,128]{3,1,2,0:T(8,128)S(1)} %copy.29), kind=kLoop, calls=%fused_computation.2 | loop fusion | flops 249600 | bytes 1996800 | tf_op jit(solution)/shard_map/concatenate | solution.py:426
  25.0 4.7 %collective-permute-start.1 = (f32[5,130,3,128]{3,1,2,0:T(8,128)}, f32[5,130,3,128]{3,1,2,0:T(8,128)}, u32[]{:S(2)}, u32[]{:S(2)}) collective-permute-start(f32[5,130,3,128]{3,1,2,0:T(8,128)} %pad_maximum_fusion.2), channel_id=1, source_target_pairs={{0,1},{1,2},{2,3},{3,4},{4,5},{5,6},{6,7},{7,8},{8,9},{9,10},{10,1... | collective-permute-start | bytes 2995208 | tf_op jit(solution)/shard_map/ppermute | solution.py:30
  29.7 0.0 copy-done.4
  29.7 0.1 stack.84
  29.8 0.0 copy-done.5
  29.8 0.0 copy-done.6
  29.8 0.1 stack.80
  29.9 0.1 stack.79
  30.0 0.1 stack.81
  30.1 0.1 stack.82
  30.1 0.1 stack.83
  30.3 0.1 copy.27
  30.4 0.1 multiply_select_fusion
  30.5 0.1 broadcast_and_fusion
  30.6 0.2 select_select_fusion.coef_ref
  30.8 0.1 pad.9.clone
  30.9 0.0 collective-permute-done.3
  30.9 0.0 collective-permute-done.4
  30.9 0.1 pad_maximum_fusion.4.own_halo_ref
  31.0 0.6 collective-permute-start.5
  31.6 0.1 copy.26
  31.8 0.3 broadcast_in_dim.65
  32.1 0.3 reshape.196.coef_ref
  32.4 0.0 copy-done.7
  32.4 0.1 pad.4.mix_ref
  33.1 0.0 copy-done
  33.1 3.3 %columns.1 = (f32[2,80,1024]{2,1,0:T(8,128)S(1)}, f32[80,128]{1,0:T(8,128)S(1)}) custom-call(f32[81]{0:T(128)S(1)} %pad.4.mix_ref, f32[2,80,1024]{2,1,0:T(8,128)S(1)} %copy-done), custom_call_target="tpu_custom_call" | custom-call | tf_op jit(solution)/shard_map/columns/pallas_call | solution.py:475
  36.4 0.9 collective-permute-done.5.other_halo_ref
  37.3 0.0 collective-permute-done.2.other_ref
  37.3 0.1 broadcast_in_dim.66.mask_ref
  37.4 1.0 %seam.1.h_ref = f32[3,32,40,128]{3,2,1,0:T(8,128)S(1)} custom-call(f32[33,32,128]{2,1,0:T(8,128)S(1)} %pack.1.own_ref, f32[33,32,128]{2,1,0:T(8,128)S(1)} %collective-permute-done.2.other_ref, f32[33,8,128]{2,1,0:T(8,128)S(1)} %pad_maximum_fusion.4.own_halo_ref, f32[33,8,128]{2,1,0:T(8,128)S(1)} %collective-permute-done.5.other_halo_ref, ...), custom_call_target="tpu_custom_call" | custom-call | tf_op jit(solution)/shard_map/seam/pallas_call | solution.py:487
  38.4 0.0 collective-permute-done
  38.4 1.6 %copy.24 = f32[5,130,3,128]{3,2,1,0:T(4,128)S(1)} copy(f32[5,130,3,128]{3,1,2,0:T(8,128)} %collective-permute-done) | data formatting | bytes 1996800 | tf_op jit(solution)/shard_map/ppermute | solution.py:30
  40.0 0.0 collective-permute-done.1
  40.0 1.6 %copy.25 = f32[5,130,3,128]{3,2,1,0:T(4,128)S(1)} copy(f32[5,130,3,128]{3,1,2,0:T(8,128)} %collective-permute-done.1) | data formatting | bytes 1996800 | tf_op jit(solution)/shard_map/ppermute | solution.py:30
  41.6 0.6 pad_maximum_fusion.halo_ref
  42.2 0.0 copy-start.1
  42.2 0.0 copy-start.2
  42.2 0.0 copy-start.3
  42.2 33.1 %march.1 = (f32[5,128,32,128]{3,2,1,0:T(8,128)}, f32[5,32,128]{2,1,0:T(8,128)S(1)}) custom-call(s32[1]{0:T(128)} %bitcast.sec_ref, f32[5,128,32,128]{3,2,1,0:T(8,128)} %x_ref.2, f32[5,130,8,128]{3,2,1,0:T(8,128)S(1)} %pad_maximum_fusion.halo_ref, f32[2,5,32,128]{3,2,1,0:T(8,128)S(1)} %pad_maximum_fusion.3.surface_ref, f32[3,32,40,128]{3,2,1,0:T(8,128)S(1)} %seam.1.h_ref, ...), custom_call_target="tpu_custom_call" | custom-call | flops 157286400 | bytes 20971520 | tf_op jit(solution)/shard_map/march/pallas_call | solution.py:189
  75.3 0.0 copy-done.1
  75.3 0.0 copy-done.2
  75.3 0.0 copy-done.3
  75.3 23.1 %remap.1 = (f32[2,80,1024]{2,1,0:T(8,128)S(1)}, f32[32,128]{1,0:T(8,128)S(1)}) custom-call(s32[1]{0:T(128)S(6)} %copy.43.extent_ref, f32[5,32,128]{2,1,0:T(8,128)S(1)} %get-tuple-element.10.flux_ref, s32[4,1024]{1,0:T(4,128)S(1)} %copy-done.2, f32[4,1024]{1,0:T(4,128)S(1)} %copy-done.3, f32[2,80,1024]{2,1,0:T(8,128)S(1)} %get-tuple-element.11.base_ref, ...), custom_call_target="tpu_custom_call" | custom-call | tf_op jit(solution)/shard_map/remap/pallas_call | solution.py:497
  98.4 0.8 copy.44
  99.2 0.6 copy.45
  (28 shorter events, 0.2 us)
Async XLA Ops:
  10.8 26.5 %collective-permute-start.2 = (f32[33,32,128]{2,1,0:T(8,128)S(1)}, f32[33,32,128]{2,1,0:T(8,128)S(1)}, u32[]{:S(2)}, u32[]{:S(2)}) collective-permute-start(f32[33,32,128]{2,1,0:T(8,128)S(1)} %pack.1.own_ref), channel_id=1, source_target_pairs={{0,16},{16,0},{1,17},{17,1},{2,18},{18,2},{3,19},{19,3},{4,20},{20... | collective-permute-start | bytes 1622024 | tf_op jit(solution)/shard_map/ppermute | solution.py:448
  13.8 17.1 %collective-permute-start.3 = (f32[33,3,128]{2,1,0:T(4,128)S(1)}, f32[33,3,128]{2,1,0:T(4,128)S(1)}, u32[]{:S(2)}, u32[]{:S(2)}) collective-permute-start(f32[33,3,128]{2,1,0:T(4,128)S(1)} %get-tuple-element.17), channel_id=1, source_target_pairs={{1,0},{2,1},{3,2},{4,3},{5,4},{6,5},{7,6},{8,7},{9,8},{10,9},{11,1... | collective-permute-start | bytes 152072 | tf_op jit(solution)/shard_map/ppermute | solution.py:30
  15.1 15.8 %collective-permute-start.4 = (f32[33,3,128]{2,1,0:T(4,128)S(1)}, f32[33,3,128]{2,1,0:T(4,128)S(1)}, u32[]{:S(2)}, u32[]{:S(2)}) collective-permute-start(f32[33,3,128]{2,1,0:T(4,128)S(1)} %get-tuple-element.18), channel_id=1, source_target_pairs={{0,1},{1,2},{2,3},{3,4},{4,5},{5,6},{6,7},{7,8},{8,9},{9,10},{10,1... | collective-permute-start | bytes 152072 | tf_op jit(solution)/shard_map/ppermute | solution.py:30
  22.4 7.3 %copy-start.4 = (f32[128]{0:T(128)S(1)}, f32[128]{0:T(128)}, u32[]{:S(2)}) copy-start(f32[128]{0:T(128)} %param.16) | copy-start | bytes 1540
  22.4 7.4 %copy-start.5 = (f32[2,128]{1,0:T(2,128)S(1)}, f32[2,128]{1,0:T(2,128)}, u32[]{:S(2)}) copy-start(f32[2,128]{1,0:T(2,128)} %param.14) | copy-start | bytes 3076
  22.4 7.4 %copy-start.6 = (f32[128]{0:T(128)S(1)}, f32[128]{0:T(128)}, u32[]{:S(2)}) copy-start(f32[128]{0:T(128)} %param.15) | copy-start | bytes 1540
  22.4 16.1 %collective-permute-start = (f32[5,130,3,128]{3,1,2,0:T(8,128)}, f32[5,130,3,128]{3,1,2,0:T(8,128)}, u32[]{:S(2)}, u32[]{:S(2)}) collective-permute-start(f32[5,130,3,128]{3,1,2,0:T(8,128)} %pad_maximum_fusion.1), channel_id=1, source_target_pairs={{1,0},{2,1},{3,2},{4,3},{5,4},{6,5},{7,6},{8,7},{9,8},{10,9},{11,1... | collective-permute-start | bytes 2995208 | tf_op jit(solution)/shard_map/ppermute | solution.py:30
  23.9 8.4 %copy-start.7 = (f32[79]{0:T(128)S(1)}, f32[79]{0:T(128)}, u32[]{:S(2)}) copy-start(f32[79]{0:T(128)} %param.22) | copy-start | bytes 952
  23.9 9.2 %copy-start = (f32[2,80,1024]{2,1,0:T(8,128)S(1)}, f32[2,80,1024]{2,1,0:T(8,128)}, u32[]{:S(2)}) copy-start(f32[2,80,1024]{2,1,0:T(8,128)} %x_ref.3) | copy-start | bytes 1966084
  25.0 15.0 %collective-permute-start.1 = (f32[5,130,3,128]{3,1,2,0:T(8,128)}, f32[5,130,3,128]{3,1,2,0:T(8,128)}, u32[]{:S(2)}, u32[]{:S(2)}) collective-permute-start(f32[5,130,3,128]{3,1,2,0:T(8,128)} %pad_maximum_fusion.2), channel_id=1, source_target_pairs={{0,1},{1,2},{2,3},{3,4},{4,5},{5,6},{6,7},{7,8},{8,9},{9,10},{10,1... | collective-permute-start | bytes 2995208 | tf_op jit(solution)/shard_map/ppermute | solution.py:30
  31.0 6.3 %collective-permute-start.5 = (f32[33,8,128]{2,1,0:T(8,128)S(1)}, f32[33,8,128]{2,1,0:T(8,128)S(1)}, u32[]{:S(2)}, u32[]{:S(2)}) collective-permute-start(f32[33,8,128]{2,1,0:T(8,128)S(1)} %pad_maximum_fusion.4.own_halo_ref), channel_id=1, source_target_pairs={{0,16},{16,0},{1,17},{17,1},{2,18},{18,2},{3,19},{19,3},{4,20},{20... | collective-permute-start | bytes 405512 | tf_op jit(solution)/shard_map/ppermute | solution.py:450
  42.2 33.1 %copy-start.1 = (f32[32,128]{1,0:T(8,128)S(1)}, f32[32,128]{1,0:T(8,128)}, u32[]{:S(2)}) copy-start(f32[32,128]{1,0:T(8,128)} %earlier_ref.1) | copy-start | bytes 49156
  42.2 33.1 %copy-start.2 = (s32[4,1024]{1,0:T(4,128)S(1)}, s32[4,1024]{1,0:T(4,128)}, u32[]{:S(2)}) copy-start(s32[4,1024]{1,0:T(4,128)} %site_ref.1) | copy-start | bytes 49156
  42.2 33.1 %copy-start.3 = (f32[4,1024]{1,0:T(4,128)S(1)}, f32[4,1024]{1,0:T(4,128)}, u32[]{:S(2)}) copy-start(f32[4,1024]{1,0:T(4,128)} %share_ref.1) | copy-start | bytes 49156
